TPU v7x, 32 devices: a whole 2x2x4 slice. The times are simulated.
32 devices in a mesh: dp: 2 (over core), row: 4 (over z), col: 4 (over y, x).
Axes of the slice: x: 2, y: 2, z: 4, core: 2. Of those that a mesh axis runs over, the one named last changes fastest.
Arguments:
- inputs: float32 [12000, 768], P(('dp', 'row', 'col')), may hold values from -6 to 6
- first_gain: float32 [768], replicated, may hold values from 0.25 to 1.75
- first_shift: float32 [768], replicated, may hold values from -3 to 3
- query_weight: bfloat16 [768, 768], P('row', 'col'), may hold values from -0.21875 to 0.21875
- query_bias: float32 [768], P('col'), may hold values from -2 to 2
- key_weight: bfloat16 [768, 768], P('row', 'col'), may hold values from -0.21875 to 0.21875
- value_weight: bfloat16 [768, 768], P('row', 'col'), may hold values from -0.21875 to 0.21875
- value_bias: float32 [768], P('col'), may hold values from -0.2 to 0.2
- out_weight: bfloat16 [768, 768], P('col', 'row'), may hold values from -4 to 4
- out_bias: float32 [768], replicated, may hold values from -2 to 2
- second_gain: float32 [768], replicated, may hold values from 0.25 to 1.75
- second_shift: float32 [768], replicated, may hold values from -3 to 3
- up_weight: bfloat16 [768, 3072], P('row', 'col'), may hold values from -0.21875 to 0.21875
- up_bias: float32 [3072], P('col'), may hold values from -3 to 3
- down_weight: bfloat16 [3072, 768], P('col', 'row'), may hold values from -0.21875 to 0.21875
- down_bias: float32 [768], replicated, may hold values from -2 to 2
- cotangent: float32 [12000, 768], P(('dp', 'row', 'col')), may hold values from -6 to 6
Outputs:
- result: float32 [12000, 768], P(('dp', 'row', 'col'))
- inputs_grad: float32 [12000, 768], P(('dp', 'row', 'col'))
- first_gain_grad: float32 [768], replicated
- first_shift_grad: float32 [768], replicated
- query_weight_grad: float32 [768, 768], P('row', 'col')
- query_bias_grad: float32 [768], P('col')
- key_weight_grad: float32 [768, 768], P('row', 'col')
- value_weight_grad: float32 [768, 768], P('row', 'col')
- value_bias_grad: float32 [768], P('col')
- out_weight_grad: float32 [768, 768], P('col', 'row')
- out_bias_grad: float32 [768], replicated
- second_gain_grad: float32 [768], replicated
- second_shift_grad: float32 [768], replicated
- up_weight_grad: float32 [768, 3072], P('row', 'col')
- up_bias_grad: float32 [3072], P('col')
- down_weight_grad: float32 [3072, 768], P('col', 'row')
- down_bias_grad: float32 [768], replicated
All inputs are finite; a program needn't handle non-finite values.
Results may differ from a plain program's by a relative error of at most 0.011.
Values may be sent and summed in bfloat16 or wider, within the bound.
A program may use at most 192 MiB of HBM per device.

v0:
```python
import math

import jax
import jax.numpy as jnp
from jax import lax
from jax.sharding import PartitionSpec as P

HEAD_DIM = 64
LENGTH = 1500


def norm_forward(stream, scale_row, shift_row):
    center = jnp.mean(stream, axis=1, keepdims=True)
    second = jnp.mean(stream * stream, axis=1, keepdims=True)
    inverse = lax.rsqrt(second - center * center + 1e-05)
    normed = (stream - center) * inverse
    return ((normed * scale_row + shift_row).astype(jnp.bfloat16), normed, inverse)


def norm_backward(upstream, normed, inverse, scale_row):
    scaled = upstream * scale_row
    back_rows = inverse * (
        scaled
        - jnp.mean(scaled, axis=1, keepdims=True)
        - normed * jnp.mean(scaled * normed, axis=1, keepdims=True)
    )
    return (back_rows, jnp.sum(upstream * normed, axis=0), jnp.sum(upstream, axis=0))


def plain_product(left_side, right_side):
    return jnp.dot(left_side, right_side, preferred_element_type=jnp.float32)


def contract_last(left_side, right_side):
    return lax.dot_general(
        left_side, right_side, (((1,), (1,)), ((), ())), preferred_element_type=jnp.float32
    )


def contract_first(left_side, right_side):
    return lax.dot_general(
        left_side, right_side, (((0,), (0,)), ((), ())), preferred_element_type=jnp.float32
    )


def gather_frames(stream_rows):
    return lax.all_gather(stream_rows, "col", axis=0, tiled=True)


def to_stream(source, weight_full, product):
    return lax.psum_scatter(product(source, weight_full), "col", scatter_dimension=0, tiled=True)


def clip_forward(bundle):
    query_rows, key_matrix_rows, value_rows = bundle
    softmax_scale = 1.0 / math.sqrt(HEAD_DIM)
    attention_scores = (
        jnp.einsum("ugj,pgj->gup", query_rows, key_matrix_rows, preferred_element_type=jnp.float32)
        * softmax_scale
    )
    highest = jnp.max(attention_scores, axis=-1, keepdims=True)
    exponent = jnp.exp(attention_scores - highest)
    summed = jnp.sum(exponent, axis=-1, keepdims=True)
    rounded_probs = (exponent / summed).astype(jnp.bfloat16)
    attended_values = jnp.einsum(
        "gqx,xgp->qgp", rounded_probs, value_rows, preferred_element_type=jnp.float32
    )
    return (attended_values, (highest + jnp.log(summed))[..., 0])


def clip_backward(bundle):
    query_rows, key_matrix_rows, value_rows, attended_values_grad, log_total = bundle
    softmax_scale = 1.0 / math.sqrt(HEAD_DIM)
    attention_scores = (
        jnp.einsum("ugj,pgj->gup", query_rows, key_matrix_rows, preferred_element_type=jnp.float32)
        * softmax_scale
    )
    normalized_score_rows = jnp.exp(attention_scores - log_total[..., None])
    rounded_probs = normalized_score_rows.astype(jnp.bfloat16)
    value_grad = jnp.einsum(
        "iog,oif->gif", rounded_probs, attended_values_grad, preferred_element_type=jnp.float32
    )
    prob_grad = jnp.einsum(
        "ugj,pgj->gup", attended_values_grad, value_rows, preferred_element_type=jnp.float32
    )
    inner_sum = jnp.sum(normalized_score_rows * prob_grad, axis=-1, keepdims=True)
    scores_gradient = (normalized_score_rows * (prob_grad - inner_sum)).astype(jnp.bfloat16)
    query_grad = (
        jnp.einsum(
            "gqx,xgp->qgp", scores_gradient, key_matrix_rows, preferred_element_type=jnp.float32
        )
        * softmax_scale
    )
    key_grad = (
        jnp.einsum("iog,oif->gif", scores_gradient, query_rows, preferred_element_type=jnp.float32)
        * softmax_scale
    )
    return (
        query_grad.astype(jnp.bfloat16),
        key_grad.astype(jnp.bfloat16),
        value_grad.astype(jnp.bfloat16),
    )


def exact_gelu(value_rows):
    return jax.nn.gelu(value_rows, approximate=False)


def per_device(
    inputs,
    first_gain,
    first_shift,
    query_weight,
    query_bias,
    key_weight,
    value_weight,
    value_bias,
    out_weight,
    out_bias,
    second_gain,
    second_shift,
    up_weight,
    up_bias,
    down_weight,
    down_bias,
    cotangent,
):
    head_cols = query_weight.shape[1]
    in_full = (
        lax.all_gather(query_weight, "row", axis=0, tiled=True),
        lax.all_gather(key_weight, "row", axis=0, tiled=True),
        lax.all_gather(value_weight, "row", axis=0, tiled=True),
        lax.all_gather(up_weight, "row", axis=0, tiled=True),
    )
    out_full = (
        lax.all_gather(out_weight, "row", axis=1, tiled=True),
        lax.all_gather(down_weight, "row", axis=1, tiled=True),
    )
    joined = jnp.concatenate([in_full[0], in_full[1], in_full[2]], axis=1)
    attn_in, first_normed, first_inverse = norm_forward(inputs, first_gain, first_shift)
    attn_gathered = gather_frames(attn_in)
    projected = jnp.dot(attn_gathered, joined, preferred_element_type=jnp.float32)
    query_rows = (projected[:, :head_cols] + query_bias).astype(jnp.bfloat16)
    key_matrix_rows = projected[:, head_cols : 2 * head_cols].astype(jnp.bfloat16)
    value_rows = (projected[:, 2 * head_cols :] + value_bias).astype(jnp.bfloat16)
    local_tokens = query_rows.shape[0]
    clip_shape = (local_tokens // LENGTH, LENGTH, head_cols // HEAD_DIM, HEAD_DIM)
    clip_queries = query_rows.reshape(clip_shape)
    clip_keys = key_matrix_rows.reshape(clip_shape)
    clip_values = value_rows.reshape(clip_shape)
    attended_values, log_total = lax.map(clip_forward, (clip_queries, clip_keys, clip_values))
    attended_values = attended_values.reshape(local_tokens, head_cols).astype(jnp.bfloat16)
    middle = inputs + (to_stream(attended_values, out_full[0], plain_product) + out_bias)
    mlp_in, second_normed, second_inverse = norm_forward(middle, second_gain, second_shift)
    mlp_gathered = gather_frames(mlp_in)
    pre_act = jnp.dot(mlp_gathered, in_full[3], preferred_element_type=jnp.float32) + up_bias
    hidden = exact_gelu(pre_act).astype(jnp.bfloat16)
    result = middle + (to_stream(hidden, out_full[1], plain_product) + down_bias)
    in_back = (
        lax.all_gather(query_weight, "row", axis=0, tiled=True),
        lax.all_gather(key_weight, "row", axis=0, tiled=True),
        lax.all_gather(value_weight, "row", axis=0, tiled=True),
        lax.all_gather(up_weight, "row", axis=0, tiled=True),
    )
    out_back = (
        lax.all_gather(out_weight, "row", axis=1, tiled=True),
        lax.all_gather(down_weight, "row", axis=1, tiled=True),
    )
    joined_back = jnp.concatenate([in_back[0], in_back[1], in_back[2]], axis=1)
    out_grad = cotangent.astype(jnp.bfloat16)
    out_gathered = gather_frames(out_grad)
    hidden_grad = contract_last(out_gathered, out_back[1])
    down_part_turned = contract_first(out_gathered, hidden)
    gelu_pullback = jax.vjp(exact_gelu, pre_act)[1]
    pre_grad = gelu_pullback(hidden_grad)[0].astype(jnp.bfloat16)
    up_part = contract_first(mlp_gathered, pre_grad)
    mlp_back = to_stream(pre_grad, in_back[3], contract_last)
    norm_rows, second_gain_part, second_shift_part = norm_backward(
        mlp_back, second_normed, second_inverse, second_gain
    )
    middle_grad = cotangent + norm_rows
    attn_grad = middle_grad.astype(jnp.bfloat16)
    attn_gathered_grad = gather_frames(attn_grad)
    attended_values_grad = contract_last(attn_gathered_grad, out_back[0])
    out_part_turned = contract_first(attn_gathered_grad, attended_values)
    attended_values_grad = attended_values_grad.astype(jnp.bfloat16).reshape(clip_shape)
    query_grad, key_grad, value_grad = lax.map(
        clip_backward, (clip_queries, clip_keys, clip_values, attended_values_grad, log_total)
    )
    query_grad = query_grad.reshape(local_tokens, head_cols)
    key_grad = key_grad.reshape(local_tokens, head_cols)
    value_grad = value_grad.reshape(local_tokens, head_cols)
    joined_grad_rows = jnp.concatenate([query_grad, key_grad, value_grad], axis=1)
    joined_part = contract_first(attn_gathered, joined_grad_rows)
    attn_back = to_stream(joined_grad_rows, joined_back, contract_last)
    norm_rows, first_gain_part, first_shift_part = norm_backward(
        attn_back, first_normed, first_inverse, first_gain
    )
    inputs_grad = middle_grad + norm_rows
    query_part = joined_part[:, :head_cols]
    key_part = joined_part[:, head_cols : 2 * head_cols]
    value_part = joined_part[:, 2 * head_cols :]
    query_bias_part = jnp.sum(query_grad, axis=0, dtype=jnp.float32)
    value_bias_part = jnp.sum(value_grad, axis=0, dtype=jnp.float32)
    up_bias_part = jnp.sum(pre_grad, axis=0, dtype=jnp.float32)
    row_blocks = (
        lax.psum_scatter(query_part, "row", scatter_dimension=0, tiled=True),
        lax.psum_scatter(key_part, "row", scatter_dimension=0, tiled=True),
        lax.psum_scatter(value_part, "row", scatter_dimension=0, tiled=True),
        lax.psum_scatter(up_part, "row", scatter_dimension=0, tiled=True),
        lax.psum_scatter(out_part_turned, "row", scatter_dimension=0, tiled=True),
        lax.psum_scatter(down_part_turned, "row", scatter_dimension=0, tiled=True),
    )
    shares = (
        lax.psum_scatter(row_blocks[0], "dp", scatter_dimension=0, tiled=True),
        lax.psum_scatter(row_blocks[1], "dp", scatter_dimension=0, tiled=True),
        lax.psum_scatter(row_blocks[2], "dp", scatter_dimension=0, tiled=True),
        lax.psum_scatter(row_blocks[3], "dp", scatter_dimension=0, tiled=True),
        lax.psum_scatter(row_blocks[4], "dp", scatter_dimension=0, tiled=True),
        lax.psum_scatter(row_blocks[5], "dp", scatter_dimension=0, tiled=True),
    )
    summed_blocks = (
        lax.all_gather(shares[0], "dp", axis=0, tiled=True),
        lax.all_gather(shares[1], "dp", axis=0, tiled=True),
        lax.all_gather(shares[2], "dp", axis=0, tiled=True),
        lax.all_gather(shares[3], "dp", axis=0, tiled=True),
        lax.all_gather(shares[4], "dp", axis=0, tiled=True),
        lax.all_gather(shares[5], "dp", axis=0, tiled=True),
    )
    (
        query_weight_grad,
        key_weight_grad,
        value_weight_grad,
        up_weight_grad,
        out_turned,
        down_turned,
    ) = summed_blocks
    out_weight_grad = jnp.transpose(out_turned)
    down_weight_grad = jnp.transpose(down_turned)
    query_bias_grad, value_bias_grad, up_bias_grad = lax.psum(
        (query_bias_part, value_bias_part, up_bias_part), ("dp", "row")
    )
    (
        first_gain_grad,
        first_shift_grad,
        out_bias_grad,
        second_gain_grad,
        second_shift_grad,
        down_bias_grad,
    ) = lax.psum(
        (
            first_gain_part,
            first_shift_part,
            jnp.sum(attn_grad, axis=0, dtype=jnp.float32),
            second_gain_part,
            second_shift_part,
            jnp.sum(out_grad, axis=0, dtype=jnp.float32),
        ),
        ("dp", "row", "col"),
    )
    return (
        result,
        inputs_grad,
        first_gain_grad,
        first_shift_grad,
        query_weight_grad,
        query_bias_grad,
        key_weight_grad,
        value_weight_grad,
        value_bias_grad,
        out_weight_grad,
        out_bias_grad,
        second_gain_grad,
        second_shift_grad,
        up_weight_grad,
        up_bias_grad,
        down_weight_grad,
        down_bias_grad,
    )


def solution(mesh):
    placed = (
        P(("dp", "row", "col"), None),
        P(),
        P(),
        P("row", "col"),
        P("col"),
        P("row", "col"),
        P("row", "col"),
        P("col"),
        P("col", "row"),
        P(),
        P(),
        P(),
        P("row", "col"),
        P("col"),
        P("col", "row"),
        P(),
        P(("dp", "row", "col"), None),
    )
    return jax.shard_map(
        per_device,
        mesh=mesh,
        in_specs=placed,
        out_specs=(
            P(("dp", "row", "col"), None),
            P(("dp", "row", "col"), None),
            P(),
            P(),
            P("row", "col"),
            P("col"),
            P("row", "col"),
            P("row", "col"),
            P("col"),
            P("col", "row"),
            P(),
            P(),
            P(),
            P("row", "col"),
            P("col"),
            P("col", "row"),
            P(),
        ),
        check_vma=False,
    )
```

profile of v0, /device:TPU:5, one launch (start us, length us, event | category | flops | bytes accessed | tf_op | source)
XLA Modules:
  0.0 911.3 jit_solution(7864940528091934121)
XLA Ops:
  13.0 13.1 %all_gather.58 = bf16[192,768]{0,1:T(8,128)(2,1)S(1)} all-gather(bf16[192,192]{0,1:T(8,128)(2,1)S(1)} %copy.53), channel_id=1, replica_groups=mesh['dp'=2,'row'=4,'col'=4] {'row'}, dimensions={1}, use_global_device_ids=true | all-gather | bytes 368640 | tf_op jit(solution)/shard_map/all_gather | solution.py:136
  26.0 11.4 %all_gather.55 = bf16[768,192]{1,0:T(8,128)(2,1)S(1)} all-gather(bf16[192,192]{1,0:T(8,128)(2,1)S(1)} %copy-done.29), channel_id=1, replica_groups=mesh['dp'=2,'row'=4,'col'=4] {'row'}, dimensions={0}, use_global_device_ids=true | all-gather | bytes 368640 | tf_op jit(solution)/shard_map/all_gather | solution.py:130
  37.5 13.0 %all_gather.56 = bf16[768,192]{1,0:T(8,128)(2,1)S(1)} all-gather(bf16[192,192]{1,0:T(8,128)(2,1)S(1)} %copy-done.30), channel_id=1, replica_groups=mesh['dp'=2,'row'=4,'col'=4] {'row'}, dimensions={0}, use_global_device_ids=true | all-gather | bytes 368640 | tf_op jit(solution)/shard_map/all_gather | solution.py:131
  50.5 12.6 %all_gather.57 = bf16[768,192]{1,0:T(8,128)(2,1)S(1)} all-gather(bf16[192,192]{1,0:T(8,128)(2,1)S(1)} %copy-done.31), channel_id=1, replica_groups=mesh['dp'=2,'row'=4,'col'=4] {'row'}, dimensions={0}, use_global_device_ids=true | all-gather | bytes 368640 | tf_op jit(solution)/shard_map/all_gather | solution.py:132
  63.0 3.8 reshape.140
  66.9 3.4 fusion.29
  70.6 11.5 %multiply_reduce_fusion.1 = (f32[3,1500]{1,0:T(4,128)S(1)}, f32[3,1500,1500]{1,2,0:T(8,128)}) fusion(bf16[1500,3,64]{0,2,1:T(8,128)(2,1)S(1)} %bitcast.80, bf16[1500,3,64]{0,2,1:T(8,128)(2,1)S(1)} %bitcast.78), kind=kOutput, calls=%fused_computation.6 | convolution fusion | flops 877495488 | bytes 28170000 | tf_op jit(solution)/shard_map/while/body/eval_jaxpr/ugj,pgj->gup/dot_general | solution.py:58
  82.1 11.8 %fusion.4 = f32[3,1500]{1,0:T(4,128)S(1)} fusion(f32[3,1500,1500]{1,2,0:T(8,128)} %get-tuple-element.155, f32[3,1500]{1,0:T(4,128)S(1)} %get-tuple-element.154), kind=kLoop, calls=%fused_computation.5 | loop fusion | flops 20245500 | bytes 27036000 | tf_op jit(solution)/shard_map/while/body/eval_jaxpr/reduce_sum | solution.py:63
  93.9 11.5 %fusion.17 = bf16[3,64,1500]{2,1,0:T(8,128)(2,1)S(1)} fusion(bf16[1500,3,64]{0,2,1:T(8,128)(2,1)S(1)} %bitcast.87, f32[3,1500,1500]{1,2,0:T(8,128)} %get-tuple-element.155, f32[3,1500]{1,0:T(4,128)S(1)} %fusion.4, f32[3,1500]{1,0:T(4,128)S(1)} %get-tuple-element.154), kind=kOutput, calls=%fused_computation.33 | convolution fusion | flops 891288000 | bytes 28188000 | tf_op jit(solution)/shard_map/while/body/eval_jaxpr/gqx,xgp->qgp/dot_general | solution.py:65
  105.5 3.0 fusion.41
  108.5 68.7 %fusion = f32[384,768]{1,0:T(8,128)S(1)} fusion(f32[1500,768]{1,0:T(8,128)} %fusion.41), kind=kCustom, calls=%all-reduce-scatter | all-reduce-scatter fusion | flops 1179649 | bytes 5788160
  177.3 3.2 collective-permute-start
  183.7 4.3 concatenate.9
  192.5 3.8 reshape.144
  196.4 34.3 %all-gather.17.cloned.1.call-done = bf16[4,375,768]{2,1,0:T(8,128)(2,1)} async-done(((bf16[1,375,768]{2,1,0:T(8,128)(2,1)}), bf16[4,375,768]{2,1,0:T(8,128)(2,1)}) %all-gather.17.cloned.1.call-update) | async-done | bytes 2304016 | tf_op jit(solution)/shard_map/all_gather | solution.py:47
  230.7 3.7 reshape.142
  234.4 27.6 %all-gather.11.cloned.1.call-done = bf16[768,768]{1,0:T(8,128)(2,1)} async-done(((bf16[192,768]{1,0:T(8,128)(2,1)}), bf16[768,768]{1,0:T(8,128)(2,1)}) %all-gather.11.cloned.1.call-update) | async-done | bytes 1179664 | tf_op jit(solution)/shard_map/all_gather | solution.py:133
  262.0 6.1 fusion.42
  268.2 24.9 %all-gather.13.cloned.1.call-done = bf16[768,768]{0,1:T(8,128)(2,1)} async-done(((bf16[768,192]{0,1:T(8,128)(2,1)}), bf16[768,768]{0,1:T(8,128)(2,1)}) %all-gather.13.cloned.1.call-update) | async-done | bytes 1179664 | tf_op jit(solution)/shard_map/all_gather | solution.py:137
  293.0 15.7 %convert_reduce_fusion = (f32[768]{0:T(1024)}, bf16[1500,768]{1,0:T(8,128)(2,1)S(1)}, f32[1500,768]{1,0:T(8,128)}) fusion(f32[1500,768]{1,0:T(8,128)} %fusion.42, f32[768]{0:T(1024)S(1)} %copy-done.43, bf16[1500,768]{1,0:T(8,128)(2,1)} %reshape.144, bf16[768,768]{0,1:T(8,128)(2,1)} %all-gather.13.cloned.1.call-done), kind=kOutput, calls=%fused_computation.12 | convolution fusion | flops 1855871232 | bytes 15009792 | tf_op jit(solution)/shard_map/dot_general | solution.py:35
  310.1 4.2 fusion.44
  314.4 57.6 %fusion.2 = f32[384,768]{1,0:T(8,128)S(1)} fusion(f32[1500,768]{1,0:T(8,128)} %fusion.44), kind=kCustom, calls=%all-reduce-scatter.2 | all-reduce-scatter fusion | flops 1179649 | bytes 5788160
  372.0 3.1 collective-permute-start.2
  375.1 3.3 collective-permute-done.2
  378.3 5.2 concatenate.11
  390.1 39.6 %all-gather.21.cloned.1.call-done = bf16[4,375,768]{2,1,0:T(8,128)(2,1)} async-done(((bf16[1,375,768]{2,1,0:T(8,128)(2,1)}), bf16[4,375,768]{2,1,0:T(8,128)(2,1)}) %all-gather.21.cloned.1.call-update) | async-done | bytes 2304016 | tf_op jit(solution)/shard_map/all_gather | solution.py:47
  429.7 3.7 reshape.146
  433.4 3.5 fusion.45
  440.3 12.3 %convert_reduce_fusion.1 = (f32[3,64]{1,0:T(4,128)S(1)}, bf16[3,64,1500]{2,1,0:T(8,128)(2,1)}) fusion(bf16[1500,3,64]{0,2,1:T(8,128)(2,1)S(1)} %bitcast.82, f32[3,1500,1500]{1,2,0:T(8,128)} %get-tuple-element.155, f32[3,1500]{1,0:T(4,128)S(1)} %log_add_fusion), kind=kOutput, calls=%fused_computation.42 | convolution fusion | flops 885113792 | bytes 28170768 | tf_op jit(solution)/shard_map/while/body/eval_jaxpr/iog,oif->gif/dot_general | solution.py:80
  452.6 17.5 %multiply_reduce_fusion = (f32[3,1500]{1,0:T(4,128)S(1)}, f32[3,1500,1500]{1,2,0:T(8,128)}) fusion(f32[3,1500,1500]{1,2,0:T(8,128)} %get-tuple-element.155, f32[3,1500]{1,0:T(4,128)S(1)} %log_add_fusion, bf16[1500,3,64]{0,2,1:T(8,128)(2,1)} %bitcast.83, bf16[1500,3,64]{0,2,1:T(8,128)(2,1)} %bitcast.88), kind=kOutput, calls=%fused_computation.1 | convolution fusion | flops 890995520 | bytes 55188000 | tf_op jit(solution)/shard_map/while/body/eval_jaxpr/ugj,pgj->gup/dot_general | solution.py:83
  470.3 24.1 %multiply_convert_fusion = bf16[3,1500,1500]{1,2,0:T(8,128)(2,1)} fusion(f32[3,1500,1500]{1,2,0:T(8,128)} %get-tuple-element.157, f32[3,1500,1500]{1,2,0:T(8,128)} %get-tuple-element.155, f32[3,1500]{1,0:T(4,128)S(1)} %get-tuple-element.156, f32[3,1500]{1,0:T(4,128)S(1)} %log_add_fusion), kind=kLoop, calls=%fused_computation | loop fusion | flops 33750000 | bytes 67536000 | tf_op jit(solution)/shard_map/while/body/eval_jaxpr/convert_element_type | solution.py:87
  494.4 9.1 fusion.16
  503.5 7.8 convert_reduce_fusion.2
  521.1 6.0 fusion.46
  527.8 4.6 multiply_convert_fusion.1
  533.7 3.5 convolution_bitcast_fusion
  537.3 3.1 copy.78
  541.7 22.4 %reduce-scatter.49.cloned.1.call-done = f32[192,192]{1,0:T(8,128)} async-done(((f32[768,192]{1,0:T(8,128)}), f32[192,192]{1,0:T(8,128)}) %reduce-scatter.49.cloned.1.call-update) | async-done | bytes 147472
  564.2 25.2 %reduce-scatter.45.cloned.1.call-done = f32[192,192]{1,0:T(8,128)} async-done(((f32[768,192]{1,0:T(8,128)}), f32[192,192]{1,0:T(8,128)}) %reduce-scatter.45.cloned.1.call-update) | async-done | bytes 147472
  589.6 6.2 fusion.43
  595.8 4.3 fusion.26
  600.2 40.0 %reduce-scatter.41.cloned.1.call-done = f32[192,768]{1,0:T(8,128)} async-done(((f32[768,768]{1,0:T(8,128)}), f32[192,768]{1,0:T(8,128)}) %reduce-scatter.41.cloned.1.call-update) | async-done | bytes 589840 | tf_op jit(solution)/shard_map/reduce_scatter | solution.py:210
  640.3 159.2 %fusion.37 = (f32[384,768]{1,0:T(8,128)}, f32[384,768]{1,0:T(8,128)}) fusion(f32[1500,768]{1,0:T(8,128)} %fusion.43, f32[1500,768]{1,0:T(8,128)} %fusion.26), kind=kCustom, calls=%all-reduce-scatter.4 | all-reduce-scatter fusion | flops 2359297 | bytes 11575808
  807.0 18.2 %all-reduce.9 = (f32[192]{0:T(256)}, f32[192]{0:T(256)}, f32[768]{0:T(1024)}) all-reduce(f32[192]{0:T(256)S(1)} %reduce_sum.190, f32[192]{0:T(256)S(1)} %reduce_sum.192, f32[768]{0:T(1024)S(1)} %copy-done.46), channel_id=1, replica_groups=mesh['dp'=2,'row'=4,'col'=4] {'dp','row'}, use_global_device_ids=true, to_apply=%region_22.23 | all-reduce | flops 1152 | bytes 9216 | tf_op jit(solution)/shard_map/psum | solution.py:240
  825.2 6.1 concatenate.12
  833.3 6.0 concatenate.10
  839.3 40.3 %all-reduce.8 = (f32[768]{0:T(1024)}, f32[768]{0:T(1024)}, f32[768]{0:T(1024)}, f32[768]{0:T(1024)}, f32[768]{0:T(1024)}, /*index=5*/f32[768]{0:T(1024)}) all-reduce(f32[768]{0:T(1024)S(1)} %get-tuple-element.115, f32[768]{0:T(1024)S(1)} %get-tuple-element.120, ...), channel_id=1, replica_groups=mesh['dp'=2,'row'=4,'col'=4] {'dp','row','col'}, use_global_device_ids=true, to_apply=%region_16.17 | all-reduce | flops 4608 | bytes 36864 | tf_op jit(solution)/shard_map/psum | solution.py:250
  883.7 4.6 all_gather.67
  (198 shorter events, 67.1 us)
Async XLA Ops:
  7.2 55.8 %all-gather.15.cloned.1.call-start = ((), (), s32[]{:S(2)}) async-start(), calls=%async_computation.18 | async-start | bytes 2887680 | tf_op jit(solution)/shard_map/all_gather | solution.py:47
  9.4 16.6 %copy-start.29 = (bf16[192,192]{1,0:T(8,128)(2,1)S(1)}, bf16[192,192]{1,0:T(8,128)(2,1)}, u32[]{:S(2)}) copy-start(bf16[192,192]{1,0:T(8,128)(2,1)} %param.20) | copy-start | bytes 221188
  11.8 25.7 %copy-start.30 = (bf16[192,192]{1,0:T(8,128)(2,1)S(1)}, bf16[192,192]{1,0:T(8,128)(2,1)}, u32[]{:S(2)}) copy-start(bf16[192,192]{1,0:T(8,128)(2,1)} %param.22) | copy-start | bytes 221188
  11.8 38.7 %copy-start.31 = (bf16[192,192]{1,0:T(8,128)(2,1)S(1)}, bf16[192,192]{1,0:T(8,128)(2,1)}, u32[]{:S(2)}) copy-start(bf16[192,192]{1,0:T(8,128)(2,1)} %param.23) | copy-start | bytes 221188
  11.8 180.7 %all-gather.19.cloned.1.call-start = ((), (), s32[]{:S(2)}) async-start(), calls=%async_computation.20 | async-start | bytes 2887680 | tf_op jit(solution)/shard_map/all_gather | solution.py:47
  12.8 217.9 %all-gather.17.cloned.1.call-start = ((), (), s32[]{:S(2)}) async-start(), calls=%async_computation.19 | async-start | bytes 2887680 | tf_op jit(solution)/shard_map/all_gather | solution.py:47
  26.0 79.5 %copy-start.13 = (bf16[192,768]{0,1:T(8,128)(2,1)}, bf16[192,768]{0,1:T(8,128)(2,1)S(1)}, u32[]{:S(2)}) copy-start(bf16[192,768]{0,1:T(8,128)(2,1)S(1)} %all_gather.58) | copy-start | bytes 884740
  37.5 29.3 %copy-start.22 = (bf16[768,192]{1,0:T(8,128)(2,1)}, bf16[768,192]{1,0:T(8,128)(2,1)S(1)}, u32[]{:S(2)}) copy-start(bf16[768,192]{1,0:T(8,128)(2,1)S(1)} %all_gather.55) | copy-start | bytes 884740
  50.5 16.3 %copy-start.24 = (bf16[768,192]{1,0:T(8,128)(2,1)}, bf16[768,192]{1,0:T(8,128)(2,1)S(1)}, u32[]{:S(2)}) copy-start(bf16[768,192]{1,0:T(8,128)(2,1)S(1)} %all_gather.56) | copy-start | bytes 884740
  70.4 11.7 %copy-start.1 = (bf16[1500,192]{0,1:T(8,128)(2,1)}, bf16[1500,192]{0,1:T(8,128)(2,1)S(1)}, u32[]{:S(2)}) copy-start(bf16[1500,192]{0,1:T(8,128)(2,1)S(1)} %slice.42) | copy-start | bytes 1728004
  70.6 11.5 %copy-start.7 = (bf16[1500,192]{0,1:T(8,128)(2,1)}, bf16[1500,192]{0,1:T(8,128)(2,1)S(1)}, u32[]{:S(2)}) copy-start(bf16[1500,192]{0,1:T(8,128)(2,1)S(1)} %get-tuple-element.144) | copy-start | bytes 1728004
  70.6 23.3 %copy-start.14 = (bf16[1500,192]{0,1:T(8,128)(2,1)}, bf16[1500,192]{0,1:T(8,128)(2,1)S(1)}, u32[]{:S(2)}) copy-start(bf16[1500,192]{0,1:T(8,128)(2,1)S(1)} %get-tuple-element.145) | copy-start | bytes 1728004
  108.5 72.0 %copy-start.49 = (u32[32]{0:T(128)S(1)}, u32[32]{0:T(128)}, u32[]{:S(2)}) copy-start(u32[32]{0:T(128)} %constant.122) | copy-start | bytes 388
  177.3 10.8 %copy-start = (f32[375,768]{1,0:T(8,128)S(1)}, f32[375,768]{1,0:T(8,128)}, u32[]{:S(2)}) copy-start(f32[375,768]{1,0:T(8,128)} %param.17) | copy-start | bytes 3456004
  177.3 10.8 %copy-start.41 = (f32[768]{0:T(1024)S(1)}, f32[768]{0:T(1024)}, u32[]{:S(2)}) copy-start(f32[768]{0:T(1024)} %param.26) | copy-start | bytes 9220
  177.3 6.4 collective-permute-start
  190.8 71.2 %all-gather.11.cloned.1.call-start = ((), (), s32[]{:S(2)}) async-start(), calls=%async_computation.12 | async-start | bytes 1474560 | tf_op jit(solution)/shard_map/all_gather | solution.py:133
  191.4 101.6 %all-gather.13.cloned.1.call-start = ((), (), s32[]{:S(2)}) async-start(), calls=%async_computation.13 | async-start | bytes 1474560 | tf_op jit(solution)/shard_map/all_gather | solution.py:137
  192.0 237.7 %all-gather.21.cloned.1.call-start = ((), (), s32[]{:S(2)}) async-start(), calls=%async_computation.21 | async-start | bytes 2887680 | tf_op jit(solution)/shard_map/all_gather | solution.py:47
  234.4 58.6 %copy-start.43 = (f32[768]{0:T(1024)S(1)}, f32[768]{0:T(1024)}, u32[]{:S(2)}) copy-start(f32[768]{0:T(1024)} %param.30) | copy-start | bytes 9220
  293.0 17.1 %copy-start.50 = (bf16[768,768]{1,0:T(8,128)(2,1)S(1)}, bf16[768,768]{1,0:T(8,128)(2,1)}, u32[]{:S(2)}) copy-start(bf16[768,768]{1,0:T(8,128)(2,1)} %all-gather.11.cloned.1.call-done) | copy-start | bytes 3538948
  372.0 6.4 collective-permute-start.2
  389.8 150.6 %reduce-scatter.37.cloned.1.call-start = ((), (), s32[]{:S(2)}) async-start(), calls=%async_computation.14 | async-start | bytes 983040 | tf_op jit(solution)/shard_map/reduce_scatter | solution.py:211
  470.0 71.1 %reduce-scatter.53.cloned.1.call-start = ((), (), s32[]{:S(2)}) async-start(), calls=%async_computation.26 | async-start | bytes 983040
  470.3 24.1 %copy-start.8 = (bf16[1500,192]{0,1:T(8,128)(2,1)S(1)}, bf16[1500,192]{0,1:T(8,128)(2,1)}, u32[]{:S(2)}) copy-start(bf16[1500,192]{0,1:T(8,128)(2,1)} %copy-done.7) | copy-start | bytes 1728004
  494.4 9.1 copy-start.2
  503.5 7.8 copy-start.17
  503.5 7.8 copy-start.15
  516.5 47.6 %reduce-scatter.49.cloned.1.call-start = ((), (), s32[]{:S(2)}) async-start(), calls=%async_computation.24 | async-start | bytes 983040
  518.8 70.7 %reduce-scatter.45.cloned.1.call-start = ((), (), s32[]{:S(2)}) async-start(), calls=%async_computation.22 | async-start | bytes 983040
  521.1 119.2 %reduce-scatter.41.cloned.1.call-start = ((), (), s32[]{:S(2)}) async-start(), calls=%async_computation.16 | async-start | bytes 2949120 | tf_op jit(solution)/shard_map/reduce_scatter | solution.py:210
  527.1 306.1 %reduce-scatter.57.cloned.1.call-start = ((), (), s32[]{:S(2)}) async-start(), calls=%async_computation.28 | async-start | bytes 2949120
  540.3 343.3 %reduce-scatter.39.cloned.1.call-start = ((), (), s32[]{:S(2)}) async-start(), calls=%async_computation.15 | async-start | bytes 294912 | tf_op jit(solution)/shard_map/reduce_scatter | solution.py:219
  541.1 347.9 %reduce-scatter.55.cloned.1.call-start = ((), (), s32[]{:S(2)}) async-start(), calls=%async_computation.27 | async-start | bytes 294912 | tf_op jit(solution)/shard_map/reduce_scatter | solution.py:217
  541.7 349.5 %reduce-scatter.51.cloned.1.call-start = ((), (), s32[]{:S(2)}) async-start(), calls=%async_computation.25 | async-start | bytes 294912 | tf_op jit(solution)/shard_map/reduce_scatter | solution.py:216
  564.1 329.2 %reduce-scatter.47.cloned.1.call-start = ((), (), s32[]{:S(2)}) async-start(), calls=%async_computation.23 | async-start | bytes 294912 | tf_op jit(solution)/shard_map/reduce_scatter | solution.py:215
  589.4 306.0 %reduce-scatter.43.cloned.1.call-start = ((), (), s32[]{:S(2)}) async-start(), calls=%async_computation.17 | async-start | bytes 884736 | tf_op jit(solution)/shard_map/reduce_scatter | solution.py:218
  640.2 166.7 %copy-start.46 = (f32[768]{0:T(1024)S(1)}, f32[768]{0:T(1024)}, u32[]{:S(2)}) copy-start(f32[768]{0:T(1024)} %get-tuple-element.138) | copy-start | bytes 9220
  640.3 257.7 %reduce-scatter.59.cloned.1.call-start = ((), (), s32[]{:S(2)}) async-start(), calls=%async_computation.29 | async-start | bytes 884736 | tf_op jit(solution)/shard_map/reduce_scatter | solution.py:220
  799.5 31.7 %copy-start.33 = (f32[768]{0:T(1024)S(1)}, f32[768]{0:T(1024)}, u32[]{:S(2)}) copy-start(f32[768]{0:T(1024)} %param.18) | copy-start | bytes 9220
  799.5 31.8 %copy-start.35 = (f32[375]{0:T(512)S(1)}, f32[375]{0:T(512)}, u32[]{:S(2)}) copy-start(f32[375]{0:T(512)} %copy-done.34) | copy-start | bytes 4504
  799.5 31.8 %copy-start.37 = (f32[375]{0:T(512)S(1)}, f32[375]{0:T(512)}, u32[]{:S(2)}) copy-start(f32[375]{0:T(512)} %copy-done.36) | copy-start | bytes 4504
  801.1 24.1 %collective-permute-start.3 = (f32[27,768]{1,0:T(8,128)}, f32[27,768]{1,0:T(8,128)}, u32[]{:S(2)}, u32[]{:S(2)}) collective-permute-start(f32[27,768]{1,0:T(8,128)} %slice.34), channel_id=1, source_target_pairs={{0,1},{1,2},{2,3},{4,5},{5,6},{6,7},{8,9},{9,10},{10,11},{12,13},{... | collective-permute-start | bytes 248840
  805.0 28.2 %collective-permute-start.1 = (f32[27,768]{1,0:T(8,128)}, f32[27,768]{1,0:T(8,128)}, u32[]{:S(2)}, u32[]{:S(2)}) collective-permute-start(f32[27,768]{1,0:T(8,128)} %slice.32), channel_id=1, source_target_pairs={{0,1},{1,2},{2,3},{4,5},{5,6},{6,7},{8,9},{9,10},{10,11},{12,13},{... | collective-permute-start | bytes 248840
  831.2 8.1 copy-start.38
  831.2 8.1 copy-start.39
  831.3 8.1 copy-start.40
  831.3 48.3 %copy-start.45 = (f32[768]{0:T(1024)S(1)}, f32[768]{0:T(1024)}, u32[]{:S(2)}) copy-start(f32[768]{0:T(1024)} %param.32) | copy-start | bytes 9220
  (25 other events, 89.3 us)
Sparse Core Ops, SparseCore 0:
  11.9 38.2 all-gather.14
  52.1 37.0 all-gather.18
  191.0 39.6 all-gather.16
  232.1 29.8 all-gather.10
  263.4 29.5 all-gather.12
  389.9 39.6 all-gather.20
  470.2 22.0 reduce-scatter.36
  516.6 21.9 reduce-scatter.52
  541.5 22.5 reduce-scatter.48
  566.8 22.5 reduce-scatter.44
  591.7 48.4 reduce-scatter.40
  642.4 47.4 reduce-scatter.56
  692.1 7.9 reduce-scatter.38
  702.2 8.7 reduce-scatter.54
  713.0 8.7 reduce-scatter.50
  723.9 8.7 reduce-scatter.46
  734.7 9.1 reduce-scatter.42
  833.4 7.7 reduce-scatter.58
where the time goes:
time: 921 us; the launch traced here: 911 us
  blocking collectives  410 us (45%)
  waiting for transfers between devices  222 us (24%)
  matrix products  130 us (14%)
  local copies, waits for them, and re-layouts  61 us (7%)
  other arithmetic  60.4 us (7%)
  between operations  16.1 us (2%)
  starting transfers between devices  12.3 us (1%)
    unnamed x3, blocking collectives  285 us
    all_gather x4, waiting for transfers between devices, gather_frames(): return lax.all_gather(stream_rows, 'col', axis=0, tiled=True)  74 us
    unnamed x126, local copies, waits for them, and re-layouts  59.5 us
    unnamed x26, waiting for transfers between devices  55.3 us
    psum x1, blocking collectives, per_device(): lax.psum((first_gain_part, first_shift_part, jnp.sum(attn_grad, axis=0, d...  40.3 us
    reduce_scatter x1, waiting for transfers between devices, per_device(): lax.psum_scatter(up_part, 'row', scatter_dimension=0, tiled=True)  40 us
    all_gather x1, waiting for transfers between devices, per_device(): lax.all_gather(up_weight, 'row', axis=0, tiled=True)  27.6 us
    dot_general x4, matrix products, contract_last(): lax.dot_general(left_side, right_side, (((1,), (1,)), ((), ())), preferre...  26.8 us
  transfers between devices with their start and end apart: 22, of which 9 were waited for; matrix products, arithmetic and copies ran while one was open for 43% of the time, Pallas kernels for 0%

commit v1 on v0

v1 whole, which is shorter than its diff:
```python
import functools

import jax
import jax.numpy as jnp
from jax import lax
from jax.experimental import pallas as pl
from jax.experimental.pallas import tpu as pltpu
from jax.sharding import PartitionSpec as P

HEAD_DIM = 64
LENGTH = 1500
LOG2E = 1.4426950408889634
SCALE = HEAD_DIM**-0.5
BLOCK = 256
F32 = jnp.float32
BF16 = jnp.bfloat16


def dims(left_dim, right_dim):
    return (((left_dim,), (right_dim,)), ((), ()))


def dot(left_side, right_side, left_dim, right_dim):
    return lax.dot_general(
        left_side, right_side, dims(left_dim, right_dim), preferred_element_type=F32
    )


def norm_stats(stream):
    center = jnp.mean(stream, axis=1, keepdims=True)
    second = jnp.mean(stream * stream, axis=1, keepdims=True)
    inverse = lax.rsqrt(second - center * center + 1e-05)
    return (stream - center) * inverse, inverse


def norm_backward(upstream, normed, inverse, scale_row):
    scaled = upstream * scale_row
    back_rows = inverse * (
        scaled
        - jnp.mean(scaled, axis=1, keepdims=True)
        - normed * jnp.mean(scaled * normed, axis=1, keepdims=True)
    )
    return back_rows, jnp.sum(upstream * normed, axis=0), jnp.sum(upstream, axis=0)


def key_bias(keys, block_rows, real_rows):
    at = lax.broadcasted_iota(jnp.int32, (keys, 1), 0)
    return jnp.where(lax.rem(at, block_rows) < real_rows, 0.0, -1e30).astype(F32)


def forward_kernel(heads, block_rows, real_rows, q_ref, k_ref, v_ref, o_ref, lse_ref):
    bias = key_bias(k_ref.shape[0], block_rows, real_rows)
    for head in range(heads):
        cols = slice(head * HEAD_DIM, (head + 1) * HEAD_DIM)
        queries, keys, values = q_ref[:, cols], k_ref[:, cols], v_ref[:, cols]
        scores = dot(keys, queries, 1, 1) * (SCALE * LOG2E) + bias
        highest = jnp.max(scores, axis=0, keepdims=True)
        exponent = jnp.exp2(scores - highest)
        summed = jnp.sum(exponent, axis=0, keepdims=True)
        probs = (exponent * (1.0 / summed)).astype(BF16)
        turned = dot(values, probs, 0, 0)
        o_ref[:, cols] = jnp.transpose(turned).astype(BF16)
        lse_ref[head : head + 1, :] = highest + jnp.log2(summed)


def backward_kernel(
    heads, block_rows, real_rows,
    q_ref, k_ref, v_ref, g_ref, lse_ref, dq_ref, dk_ref, dv_ref, dk_sum, dv_sum,
):
    step = pl.program_id(0)

    @pl.when(step == 0)
    def _():
        dk_sum[...] = jnp.zeros_like(dk_sum)
        dv_sum[...] = jnp.zeros_like(dv_sum)

    bias = key_bias(k_ref.shape[0], block_rows, real_rows)
    for head in range(heads):
        cols = slice(head * HEAD_DIM, (head + 1) * HEAD_DIM)
        queries, keys, values = q_ref[:, cols], k_ref[:, cols], v_ref[:, cols]
        grads = g_ref[:, cols]
        scores = dot(keys, queries, 1, 1) * (SCALE * LOG2E) + bias
        probs = jnp.exp2(scores - lse_ref[head : head + 1, :])
        prob_grad = dot(values, grads, 1, 1)
        inner = jnp.sum(probs * prob_grad, axis=0, keepdims=True)
        score_grad = (probs * (prob_grad - inner)).astype(BF16)
        dv_sum[head] += dot(probs.astype(BF16), grads, 1, 0)
        dk_sum[head] += dot(score_grad, queries, 1, 0)
        turned = dot(keys, score_grad, 0, 0)
        dq_ref[:, cols] = (jnp.transpose(turned) * SCALE).astype(BF16)

    @pl.when(step == pl.num_programs(0) - 1)
    def _():
        for head in range(heads):
            cols = slice(head * HEAD_DIM, (head + 1) * HEAD_DIM)
            dk_ref[:, cols] = (dk_sum[head] * SCALE).astype(BF16)
            dv_ref[:, cols] = dv_sum[head].astype(BF16)


def attention_forward(q, k, v, block_rows, real_rows):
    tokens, width = q.shape
    heads = width // HEAD_DIM
    part = pl.BlockSpec((BLOCK, width), lambda i: (i, 0))
    whole = pl.BlockSpec((tokens, width), lambda i: (0, 0))
    return pl.pallas_call(
        functools.partial(forward_kernel, heads, block_rows, real_rows),
        grid=(tokens // BLOCK,),
        in_specs=[part, whole, whole],
        out_specs=[part, pl.BlockSpec((8, BLOCK), lambda i: (0, i))],
        out_shape=[
            jax.ShapeDtypeStruct((tokens, width), BF16),
            jax.ShapeDtypeStruct((8, tokens), F32),
        ],
        compiler_params=pltpu.CompilerParams(vmem_limit_bytes=40 * 1024 * 1024),
        cost_estimate=pl.CostEstimate(
            flops=16 * tokens * tokens * width,
            bytes_accessed=8 * tokens * width,
            transcendentals=heads * tokens * tokens,
        ),
        name="attention_forward",
    )(q, k, v)


def attention_backward(q, k, v, grads, lse, block_rows, real_rows):
    tokens, width = q.shape
    heads = width // HEAD_DIM
    part = pl.BlockSpec((BLOCK, width), lambda i: (i, 0))
    whole = pl.BlockSpec((tokens, width), lambda i: (0, 0))
    shape = jax.ShapeDtypeStruct((tokens, width), BF16)
    return pl.pallas_call(
        functools.partial(backward_kernel, heads, block_rows, real_rows),
        grid=(tokens // BLOCK,),
        in_specs=[part, whole, whole, part, pl.BlockSpec((8, BLOCK), lambda i: (0, i))],
        out_specs=[part, whole, whole],
        out_shape=[shape, shape, shape],
        scratch_shapes=[
            pltpu.VMEM((heads, tokens, HEAD_DIM), F32),
            pltpu.VMEM((heads, tokens, HEAD_DIM), F32),
        ],
        compiler_params=pltpu.CompilerParams(vmem_limit_bytes=40 * 1024 * 1024),
        cost_estimate=pl.CostEstimate(
            flops=40 * tokens * tokens * width,
            bytes_accessed=14 * tokens * width,
            transcendentals=heads * tokens * tokens,
        ),
        name="attention_backward",
    )(q, k, v, grads, lse)


def swap(block, axis, size, step):
    return lax.ppermute(block, axis, [(i, i ^ step) for i in range(size)])


def few(size):
    return size <= 8 and size & (size - 1) == 0


def tree(terms):
    while len(terms) > 1:
        terms = [terms[i] + terms[i + 1] for i in range(0, len(terms), 2)]
    return terms[0]


def spread(block, axis, size):
    return [block] + [swap(block, axis, size, j) for j in range(1, size)]


def exchange(blocks, axis, size):
    return [blocks[0]] + [swap(blocks[j], axis, size, j) for j in range(1, size)]


def sum_blocks(make, axis, size):
    sent = {j: swap(make(j).astype(BF16), axis, size, j) for j in reversed(range(1, size))}
    return tree([make(0)] + [sent[j].astype(F32) for j in range(1, size)])


def sum_all(vector, axis, size):
    if few(size):
        return tree(spread(vector, axis, size))
    return lax.psum(vector, axis)


def sum_weight(part, rows, dps):
    depth, width = part.shape
    if dps != 2:
        own = lax.psum_scatter(part, "row", scatter_dimension=0, tiled=True)
        return lax.psum(own, "dp")
    half = depth // rows // 2
    first = lax.axis_index("dp") == 0
    view = part.reshape(rows, 2, half, width)
    mine = jnp.where(first, view[:, 0], view[:, 1])
    other = jnp.where(first, view[:, 1], view[:, 0]).astype(BF16)
    total = mine + swap(other, "dp", 2, 1).astype(F32)
    if few(rows):
        me = lax.axis_index("row")
        pick = lambda j: lax.dynamic_index_in_dim(total, jnp.bitwise_xor(me, j), 0, False)
        total = sum_blocks(pick, "row", rows)
    else:
        total = lax.psum_scatter(total, "row", scatter_dimension=0, tiled=True)[0]
    theirs = swap(total, "dp", 2, 1)
    return jnp.where(
        first,
        jnp.concatenate([total, theirs], axis=0),
        jnp.concatenate([theirs, total], axis=0),
    )


def per_device(
    cols, rows, dps,
    inputs, first_gain, first_shift, query_weight, query_bias, key_weight, value_weight,
    value_bias, out_weight, out_bias, second_gain, second_shift, up_weight, up_bias,
    down_weight, down_bias, cotangent,
):
    real = inputs.shape[0]
    held = -(-real // 128) * 128
    width = inputs.shape[1]
    head_cols = query_weight.shape[1]
    assert real * cols == LENGTH and cols & (cols - 1) == 0
    fill = ((0, held - real), (0, 0))
    padded = jnp.pad(inputs, fill)
    cotangent = jnp.pad(cotangent, fill)

    def block(array, j):
        return array[j * held : (j + 1) * held]

    def join(blocks):
        return jnp.concatenate(blocks, axis=0)

    joined = lax.all_gather(
        jnp.concatenate([query_weight, key_weight, value_weight], axis=1), "row", axis=0, tiled=True
    )
    rest = lax.all_gather(
        jnp.concatenate([out_weight.T, up_weight, down_weight.T], axis=1), "row", axis=0, tiled=True
    )
    out_turned = rest[:, :head_cols]
    hidden_cols = up_weight.shape[1]
    up_full = rest[:, head_cols : head_cols + hidden_cols]
    down_turned = rest[:, head_cols + hidden_cols :]

    first_normed, first_inverse = norm_stats(padded)
    attn_in = (first_normed * first_gain + first_shift).astype(BF16)
    attn_all = join(spread(attn_in, "col", cols))
    projected = dot(attn_all, joined, 1, 0)
    queries = (projected[:, :head_cols] + query_bias).astype(BF16)
    keys = projected[:, head_cols : 2 * head_cols].astype(BF16)
    values = (projected[:, 2 * head_cols :] + value_bias).astype(BF16)

    out_full = jnp.concatenate(spread(out_turned, "col", cols), axis=1)
    out_grad = cotangent.astype(BF16)
    out_all = join(spread(out_grad, "col", cols))

    attended, lse = attention_forward(queries, keys, values, held, real)
    attended_own = jnp.concatenate(
        exchange([block(attended, j) for j in range(cols)], "col", cols), axis=1
    )
    middle = padded + (dot(attended_own, out_full, 1, 1) + out_bias)
    second_normed, second_inverse = norm_stats(middle)
    mlp_in = (second_normed * second_gain + second_shift).astype(BF16)
    mlp_all = join(spread(mlp_in, "col", cols))
    pre_act = dot(mlp_all, up_full, 1, 0) + up_bias
    hidden_grad = dot(out_all, down_turned, 1, 0)
    below = 0.5 * (1.0 + lax.erf(pre_act * (0.5**0.5)))
    slope = below + pre_act * (jnp.exp(-0.5 * pre_act * pre_act) * 0.3989422804014327)
    hidden = (pre_act * below).astype(BF16)
    pre_grad = (hidden_grad * slope).astype(BF16)
    mlp_back = sum_blocks(lambda j: dot(block(pre_grad, j), up_full, 1, 1), "col", cols)
    norm_rows, second_gain_part, second_shift_part = norm_backward(
        mlp_back, second_normed, second_inverse, second_gain
    )
    middle_grad = cotangent + norm_rows
    attn_grad = middle_grad.astype(BF16)
    attended_grad_own = dot(attn_grad, out_full, 1, 0).astype(BF16)
    attended_grad = join(
        exchange(
            [attended_grad_own[:, j * head_cols : (j + 1) * head_cols] for j in range(cols)],
            "col",
            cols,
        )
    )
    query_grad, key_grad, value_grad = attention_backward(
        queries, keys, values, attended_grad, lse, held, real
    )

    hidden_late, _ = lax.optimization_barrier((hidden, mlp_back))
    result = middle + (
        sum_blocks(lambda j: dot(block(hidden_late, j), down_turned, 1, 1), "col", cols) + down_bias
    )
    up_part = dot(mlp_all, pre_grad, 0, 0)
    down_part = dot(out_all, hidden, 0, 0)
    mlp_sum = sum_weight(jnp.concatenate([up_part, down_part], axis=1), rows, dps)
    out_part = sum_blocks(
        lambda j: dot(attn_grad, attended_own[:, j * head_cols : (j + 1) * head_cols], 0, 0),
        "col",
        cols,
    )
    out_sum = sum_weight(out_part, rows, dps)
    up_bias_part = jnp.sum(pre_grad, axis=0, dtype=F32)
    early = jnp.concatenate([
        second_gain_part,
        second_shift_part,
        jnp.sum(attn_grad, axis=0, dtype=F32),
        jnp.sum(out_grad, axis=0, dtype=F32),
    ])
    early = jnp.concatenate([sum_all(early, "col", cols), up_bias_part])
    early = sum_all(sum_all(early, "row", rows), "dp", dps)

    grad_rows = jnp.concatenate([query_grad, key_grad, value_grad], axis=1)
    attn_back = sum_blocks(lambda j: dot(block(grad_rows, j), joined, 1, 1), "col", cols)
    qkv_sum = sum_weight(dot(attn_all, grad_rows, 0, 0), rows, dps)
    norm_rows, first_gain_part, first_shift_part = norm_backward(
        attn_back, first_normed, first_inverse, first_gain
    )
    inputs_grad = middle_grad + norm_rows
    late = sum_all(jnp.concatenate([first_gain_part, first_shift_part]), "col", cols)
    late = jnp.concatenate([
        late,
        jnp.sum(query_grad, axis=0, dtype=F32),
        jnp.sum(value_grad, axis=0, dtype=F32),
    ])
    late = sum_all(sum_all(late, "row", rows), "dp", dps)

    return (
        result[:real],
        inputs_grad[:real],
        late[:width],
        late[width : 2 * width],
        qkv_sum[:, :head_cols],
        late[2 * width : 2 * width + head_cols],
        qkv_sum[:, head_cols : 2 * head_cols],
        qkv_sum[:, 2 * head_cols :],
        late[2 * width + head_cols :],
        out_sum.T,
        early[2 * width : 3 * width],
        early[:width],
        early[width : 2 * width],
        mlp_sum[:, :hidden_cols],
        early[4 * width :],
        mlp_sum[:, hidden_cols:].T,
        early[3 * width : 4 * width],
    )


def solution(mesh):
    stream = P(("dp", "row", "col"), None)
    inward, outward = P("row", "col"), P("col", "row")
    return jax.shard_map(
        functools.partial(
            per_device, mesh.shape["col"], mesh.shape["row"], mesh.shape["dp"]
        ),
        mesh=mesh,
        in_specs=(
            stream, P(), P(), inward, P("col"), inward, inward, P("col"), outward, P(), P(), P(),
            inward, P("col"), outward, P(), stream,
        ),
        out_specs=(
            stream, stream, P(), P(), inward, P("col"), inward, inward, P("col"), outward, P(),
            P(), P(), inward, P("col"), outward, P(),
        ),
        check_vma=False,
    )
```

time: 921 us -> 372 us (0.40)
  blocking collectives: 410 us -> 29.5 us
  waiting for transfers between devices: 222 us -> 107 us
  matrix products: 130 us -> 51.8 us
  Pallas kernels: 0 us -> 47 us
  starting transfers between devices: 12.3 us -> 58.7 us
  other arithmetic: 60.4 us -> 25.5 us
  local copies, waits for them, and re-layouts: 61 us -> 30.3 us
    unnamed x3 -> x0, blocking collectives: 285 us -> none
    all_gather x6 -> x1, waiting for transfers between devices: 126 us -> 2.15 us  [per_device(): lax.all_gather(jnp.concatenate([out_weight.T, up_weight, down_weight.T],...]
    ppermute x0 -> x59, waiting for transfers between devices: none -> 105 us  [swap(): return lax.ppermute(block, axis, [(i, i ^ step) for i in range(size)])]
    dot_general x18 -> x24, matrix products: 130 us -> 51.8 us  [dot(): lax.dot_general(left_side, right_side, dims(left_dim, right_dim), preferr...]
    ppermute x0 -> x59, starting transfers between devices: none -> 58.7 us  [swap(): return lax.ppermute(block, axis, [(i, i ^ step) for i in range(size)])]
    psum x2 -> x0, blocking collectives: 58.5 us -> none  [the longest x1 40.3 us: per_device(): lax.psum((first_gain_part, first_shift_part, jnp.sum(attn_grad, axis=0, d...]
    unnamed x26 -> x1, waiting for transfers between devices: 55.3 us -> 0.02 us
    unnamed x126 -> x122, local copies, waits for them, and re-layouts: 59.5 us -> 7.81 us
  transfers between devices with their start and end apart: 22 -> 60, of which waited for: 9 -> 26; matrix products, arithmetic and copies ran while one was open for 43% -> 25% of each run, Pallas kernels for 0% -> 13%
where the time goes in v1:
time: 372 us; the launch traced here: 365 us
  waiting for transfers between devices  107 us (29%)
  starting transfers between devices  58.7 us (16%)
  matrix products  51.8 us (14%)
  Pallas kernels  47 us (13%)
  local copies, waits for them, and re-layouts  30.3 us (8%)
  blocking collectives  29.5 us (8%)
  other arithmetic  25.5 us (7%)
  between operations  15.2 us (4%)
    ppermute x59, waiting for transfers between devices, swap(): return lax.ppermute(block, axis, [(i, i ^ step) for i in range(size)])  105 us
    ppermute x59, starting transfers between devices, swap(): return lax.ppermute(block, axis, [(i, i ^ step) for i in range(size)])  58.7 us
    dot_general x24, matrix products, dot(): lax.dot_general(left_side, right_side, dims(left_dim, right_dim), preferr...  51.8 us
    all_gather x1, blocking collectives, per_device(): lax.all_gather(jnp.concatenate([query_weight, key_weight, value_weight],...  29.5 us
    pallas_call x1, Pallas kernels, attention_backward(): pl.pallas_call(functools.partial(backward_kernel, heads, block_rows, real...  24.7 us
    pallas_call x1, Pallas kernels, attention_forward(): pl.pallas_call(functools.partial(forward_kernel, heads, block_rows, real_...  22.3 us
    unnamed x122, local copies, waits for them, and re-layouts  7.81 us
  transfers between devices with their start and end apart: 60, of which 26 were waited for; matrix products, arithmetic and copies ran while one was open for 25% of the time, Pallas kernels for 13%

profile of v1, /device:TPU:5, one launch (start us, length us, event | category | flops | bytes accessed | tf_op | source)
XLA Modules:
  0.0 365.2 jit_solution(1281937217655245387)
XLA Ops:
  8.3 2.3 concatenate.63
  14.0 29.5 %all_gather.6 = bf16[768,576]{1,0:T(8,128)(2,1)S(1)} all-gather(bf16[192,576]{1,0:T(8,128)(2,1)S(1)} %pad_maximum_fusion.13), channel_id=1, replica_groups=mesh['dp'=2,'row'=4,'col'=4] {'row'}, dimensions={0}, use_global_device_ids=true | all-gather | bytes 1105920 | tf_op jit(solution)/shard_map/all_gather | solution.py:229
  47.3 1.7 copy.79
  49.1 1.6 copy.77
  52.1 1.7 add_convert_fusion
  53.7 22.3 %attention_forward.1 = (bf16[1536,192]{1,0:T(8,128)(2,1)S(1)}, f32[8,1536]{1,0:T(8,128)S(1)}) custom-call(bf16[1536,192]{1,0:T(8,128)(2,1)S(1)} %get-tuple-element.96.q_ref, bf16[1536,192]{1,0:T(8,128)(2,1)S(1)} %copy.78.k_ref, bf16[1536,192]{1,0:T(8,128)(2,1)S(1)} %get-tuple-element.95.v_ref), custom_call_target="tpu_custom_call" | custom-call | flops 7247757312 | bytes 2359296 | tf_op jit(solution)/shard_map/attention_forward/pallas_call | solution.py:105
  77.9 2.2 all-gather.2.cloned.1.call-done
  85.2 22.6 %collective-permute-done.4 = bf16[384,192]{1,0:T(8,128)(2,1)S(1)} collective-permute-done((bf16[384,192]{1,0:T(8,128)(2,1)S(1)}, bf16[384,192]{1,0:T(8,128)(2,1)S(1)}, u32[]{:S(2)}, u32[]{:S(2)}) %collective-permute-start.4) | collective-permute-done | bytes 147488 | tf_op jit(solution)/shard_map/ppermute | solution.py:151
  107.9 3.0 fusion.83
  117.1 10.7 %collective-permute-done.11 = bf16[384,768]{1,0:T(8,128)(2,1)} collective-permute-done((bf16[384,768]{1,0:T(8,128)(2,1)S(1)}, bf16[384,768]{1,0:T(8,128)(2,1)}, u32[]{:S(2)}, u32[]{:S(2)}) %collective-permute-start.11) | collective-permute-done | bytes 589856 | tf_op jit(solution)/shard_map/ppermute | solution.py:151
  127.8 14.2 %collective-permute-done.10 = bf16[384,768]{1,0:T(8,128)(2,1)} collective-permute-done((bf16[384,768]{1,0:T(8,128)(2,1)S(1)}, bf16[384,768]{1,0:T(8,128)(2,1)}, u32[]{:S(2)}, u32[]{:S(2)}) %collective-permute-start.10) | collective-permute-done | bytes 589856 | tf_op jit(solution)/shard_map/ppermute | solution.py:151
  142.0 5.8 %multiply_convert_fusion = (bf16[1536,768]{1,0:T(8,128)(2,1)S(1)}, f32[1536,768]{1,0:T(8,128)S(1)}) fusion(f32[768]{0:T(1024)S(1)} %copy-done.53, bf16[768,1728]{1,0:T(8,128)(2,1)} %all-gather.2.cloned.1.call-done, bf16[384,768]{1,0:T(8,128)(2,1)} %collective-permute-done.11, bf16[384,768]{1,0:T(8,128)(2,1)} %collective-permute-done.10, ...), kind=kOutput, calls=%fused_computation.9 | convolution fusion | flops 1828454400 | bytes 10619904 | tf_op jit(solution)/shard_map/dot_general | solution.py:24
  147.8 5.3 %collective-permute-done.14 = bf16[384,768]{1,0:T(8,128)(2,1)} collective-permute-done((bf16[384,768]{1,0:T(8,128)(2,1)}, bf16[384,768]{1,0:T(8,128)(2,1)}, u32[]{:S(2)}, u32[]{:S(2)}) %collective-permute-start.14) | collective-permute-done | bytes 589856 | tf_op jit(solution)/shard_map/ppermute | solution.py:151
  153.1 13.4 %collective-permute-done.13 = bf16[384,768]{1,0:T(8,128)(2,1)} collective-permute-done((bf16[384,768]{1,0:T(8,128)(2,1)}, bf16[384,768]{1,0:T(8,128)(2,1)}, u32[]{:S(2)}, u32[]{:S(2)}) %collective-permute-start.13) | collective-permute-done | bytes 589856 | tf_op jit(solution)/shard_map/ppermute | solution.py:151
  166.5 6.7 %convert_reduce_fusion = (f32[768]{0:T(1024)S(1)}, bf16[1536,768]{1,0:T(8,128)(2,1)S(1)}) fusion(f32[1536,768]{1,0:T(8,128)S(1)} %get-tuple-element.91, f32[768]{0:T(1024)S(1)} %copy-done.53, bf16[768,1728]{1,0:T(8,128)(2,1)S(1)} %copy-done.27, bf16[384,768]{1,0:T(8,128)(2,1)} %collective-permute-done.14, bf16[384,768]{1,0:T(8,128)(2,1)} %collective-permute-done.13, ...), kind=kOutput, calls=%fused_computation.8 | convolution fusion | flops 1836711168 | bytes 10624000 | tf_op jit(solution)/shard_map/dot_general | solution.py:24
  180.6 3.6 fusion.56
  184.2 3.6 fusion.55
  187.8 2.5 pad_maximum_fusion
  190.3 6.4 %copy.71 = f32[768,1536]{1,0:T(8,128)} copy(f32[768,1536]{0,1:T(8,128)} %pad_maximum_fusion) | data formatting | bytes 9437184 | tf_op jit(solution)/shard_map/concatenate | solution.py:290
  196.8 3.7 %fusion.9 = bf16[4,96,1536]{2,1,0:T(8,128)(2,1)} fusion(f32[4,2,96,1536]{3,2,1,0:T(8,128)} %bitcast.103, pred[]{:T(512)S(6)} %eq.2), kind=kLoop, calls=%fused_computation.38 | loop fusion | flops 589824 | bytes 3538945 | tf_op jit(solution)/shard_map/convert_element_type | solution.py:192
  201.8 2.1 collective-permute-done.16
  203.9 3.2 multiply_reduce_fusion
  214.4 1.8 fusion.19
  222.4 3.0 collective-permute-start.52
  228.4 3.0 collective-permute-start.53
  234.4 2.7 collective-permute-done.22
  238.9 24.7 %attention_backward.1 = (bf16[1536,192]{1,0:T(8,128)(2,1)S(1)}, bf16[1536,192]{1,0:T(8,128)(2,1)S(1)}, bf16[1536,192]{1,0:T(8,128)(2,1)S(1)}) custom-call(bf16[1536,192]{1,0:T(8,128)(2,1)S(1)} %copy-done.1, bf16[1536,192]{1,0:T(8,128)(2,1)S(1)} %copy.78.k_ref, bf16[1536,192]{1,0:T(8,128)(2,1)S(1)} %get-tuple-element.95.v_ref, ...), custom_call_target="tpu_custom_call" | custom-call | flops 18119393280 | bytes 4128768 | tf_op jit(solution)/shard_map/attention_backward/pallas_call | solution.py:130
  265.2 3.4 fusion.57
  271.8 2.0 reshape.129
  273.8 2.2 fusion.85
  276.0 2.3 collective-permute-start.42
  279.5 3.0 collective-permute-start.45
  294.5 2.8 collective-permute-done.19
  298.5 5.9 %collective-permute-done.18 = bf16[384,768]{1,0:T(8,128)(2,1)S(1)} collective-permute-done((bf16[384,768]{1,0:T(8,128)(2,1)S(1)}, bf16[384,768]{1,0:T(8,128)(2,1)S(1)}, u32[]{:S(2)}, u32[]{:S(2)}) %collective-permute-start.18) | collective-permute-done | bytes 589856 | tf_op jit(solution)/shard_map/ppermute | solution.py:151
  304.4 1.7 collective-permute-start.37
  306.0 2.4 slice_add_fusion.1
  308.5 1.8 fusion.7
  310.4 1.9 collective-permute-start.35
  313.2 4.8 %collective-permute-done.36 = bf16[96,576]{1,0:T(8,128)(2,1)S(1)} collective-permute-done((bf16[96,576]{1,0:T(8,128)(2,1)S(1)}, bf16[96,576]{1,0:T(8,128)(2,1)S(1)}, u32[]{:S(2)}, u32[]{:S(2)}) %collective-permute-start.36) | collective-permute-done | bytes 110624 | tf_op jit(solution)/shard_map/ppermute | solution.py:151
  318.0 1.7 collective-permute-start.57
  320.5 2.1 collective-permute-done.25
  322.6 7.2 %collective-permute-done.24 = bf16[384,768]{1,0:T(8,128)(2,1)S(1)} collective-permute-done((bf16[384,768]{1,0:T(8,128)(2,1)S(1)}, bf16[384,768]{1,0:T(8,128)(2,1)S(1)}, u32[]{:S(2)}, u32[]{:S(2)}) %collective-permute-start.24) | collective-permute-done | bytes 589856 | tf_op jit(solution)/shard_map/ppermute | solution.py:151
  329.8 2.9 fusion.82
  339.6 1.9 collective-permute-start.32
  342.2 2.1 collective-permute-done.31
  344.3 3.6 collective-permute-start.38
  348.2 2.9 slice_add_fusion
  353.1 2.2 collective-permute-start.58
  (283 shorter events, 85.9 us)
Async XLA Ops:
  7.2 72.8 %all-gather.2.cloned.1.call-start = ((), (), s32[]{:S(2)}) async-start(), calls=%async_computation | async-start | bytes 3440640 | tf_op jit(solution)/shard_map/all_gather | solution.py:232
  11.2 32.4 %collective-permute-start.2 = (bf16[384,768]{1,0:T(8,128)(2,1)S(1)}, bf16[384,768]{1,0:T(8,128)(2,1)S(1)}, u32[]{:S(2)}, u32[]{:S(2)}) collective-permute-start(bf16[384,768]{1,0:T(8,128)(2,1)S(1)} %add_convert_fusion.3), channel_id=1, source_target_pairs={{0,3},{1,2},{2,1},{3,0},{4,7},{5,6},{6,5},{7,4},{8,11},{9,10},{10,... | collective-permute-start | bytes 1769480 | tf_op jit(solution)/shard_map/ppermute | solution.py:151
  12.4 31.2 %collective-permute-start.1 = (bf16[384,768]{1,0:T(8,128)(2,1)S(1)}, bf16[384,768]{1,0:T(8,128)(2,1)S(1)}, u32[]{:S(2)}, u32[]{:S(2)}) collective-permute-start(bf16[384,768]{1,0:T(8,128)(2,1)S(1)} %add_convert_fusion.3), channel_id=1, source_target_pairs={{0,2},{1,3},{2,0},{3,1},{4,6},{5,7},{6,4},{7,5},{8,10},{9,11},{10,... | collective-permute-start | bytes 1769480 | tf_op jit(solution)/shard_map/ppermute | solution.py:151
  13.6 29.9 %collective-permute-start = (bf16[384,768]{1,0:T(8,128)(2,1)S(1)}, bf16[384,768]{1,0:T(8,128)(2,1)S(1)}, u32[]{:S(2)}, u32[]{:S(2)}) collective-permute-start(bf16[384,768]{1,0:T(8,128)(2,1)S(1)} %add_convert_fusion.3), channel_id=1, source_target_pairs={{0,1},{1,0},{2,3},{3,2},{4,5},{5,4},{6,7},{7,6},{8,9},{9,8},{10,11... | collective-permute-start | bytes 1769480 | tf_op jit(solution)/shard_map/ppermute | solution.py:151
  76.8 7.2 %collective-permute-start.5 = (bf16[384,192]{1,0:T(8,128)(2,1)}, bf16[384,192]{1,0:T(8,128)(2,1)}, u32[]{:S(2)}, u32[]{:S(2)}) collective-permute-start(bf16[384,192]{1,0:T(8,128)(2,1)} %get-tuple-element.63), channel_id=1, source_target_pairs={{0,3},{1,2},{2,1},{3,0},{4,7},{5,6},{6,5},{7,4},{8,11},{9,10},{10,... | collective-permute-start | bytes 442376 | tf_op jit(solution)/shard_map/ppermute | solution.py:151
  81.1 26.8 %collective-permute-start.8 = (bf16[768,192]{1,0:T(8,128)(2,1)S(1)}, bf16[768,192]{1,0:T(8,128)(2,1)S(1)}, u32[]{:S(2)}, u32[]{:S(2)}) collective-permute-start(bf16[768,192]{1,0:T(8,128)(2,1)S(1)} %slice.202), channel_id=1, source_target_pairs={{0,3},{1,2},{2,1},{3,0},{4,7},{5,6},{6,5},{7,4},{8,11},{9,10},{10,... | collective-permute-start | bytes 884744 | tf_op jit(solution)/shard_map/ppermute | solution.py:151
  82.3 25.5 %collective-permute-start.7 = (bf16[768,192]{1,0:T(8,128)(2,1)S(1)}, bf16[768,192]{1,0:T(8,128)(2,1)S(1)}, u32[]{:S(2)}, u32[]{:S(2)}) collective-permute-start(bf16[768,192]{1,0:T(8,128)(2,1)S(1)} %slice.202), channel_id=1, source_target_pairs={{0,2},{1,3},{2,0},{3,1},{4,6},{5,7},{6,4},{7,5},{8,10},{9,11},{10,... | collective-permute-start | bytes 884744 | tf_op jit(solution)/shard_map/ppermute | solution.py:151
  83.6 24.3 %collective-permute-start.6 = (bf16[768,192]{1,0:T(8,128)(2,1)S(1)}, bf16[768,192]{1,0:T(8,128)(2,1)S(1)}, u32[]{:S(2)}, u32[]{:S(2)}) collective-permute-start(bf16[768,192]{1,0:T(8,128)(2,1)S(1)} %slice.202), channel_id=1, source_target_pairs={{0,1},{1,0},{2,3},{3,2},{4,5},{5,4},{6,7},{7,6},{8,9},{9,8},{10,11... | collective-permute-start | bytes 884744 | tf_op jit(solution)/shard_map/ppermute | solution.py:151
  83.8 24.0 %collective-permute-start.4 = (bf16[384,192]{1,0:T(8,128)(2,1)S(1)}, bf16[384,192]{1,0:T(8,128)(2,1)S(1)}, u32[]{:S(2)}, u32[]{:S(2)}) collective-permute-start(bf16[384,192]{1,0:T(8,128)(2,1)S(1)} %get-tuple-element.64), channel_id=1, source_target_pairs={{0,2},{1,3},{2,0},{3,1},{4,6},{5,7},{6,4},{7,5},{8,10},{9,11},{10,... | collective-permute-start | bytes 442376 | tf_op jit(solution)/shard_map/ppermute | solution.py:151
  84.0 23.8 %collective-permute-start.3 = (bf16[384,192]{1,0:T(8,128)(2,1)S(1)}, bf16[384,192]{1,0:T(8,128)(2,1)S(1)}, u32[]{:S(2)}, u32[]{:S(2)}) collective-permute-start(bf16[384,192]{1,0:T(8,128)(2,1)S(1)} %get-tuple-element.65), channel_id=1, source_target_pairs={{0,1},{1,0},{2,3},{3,2},{4,5},{5,4},{6,7},{7,6},{8,9},{9,8},{10,11... | collective-permute-start | bytes 442376 | tf_op jit(solution)/shard_map/ppermute | solution.py:151
  112.3 15.5 %collective-permute-start.11 = (bf16[384,768]{1,0:T(8,128)(2,1)S(1)}, bf16[384,768]{1,0:T(8,128)(2,1)}, u32[]{:S(2)}, u32[]{:S(2)}) collective-permute-start(bf16[384,768]{1,0:T(8,128)(2,1)S(1)} %add_convert_fusion.2), channel_id=1, source_target_pairs={{0,3},{1,2},{2,1},{3,0},{4,7},{5,6},{6,5},{7,4},{8,11},{9,10},{10,... | collective-permute-start | bytes 1769480 | tf_op jit(solution)/shard_map/ppermute | solution.py:151
  113.5 28.5 %collective-permute-start.10 = (bf16[384,768]{1,0:T(8,128)(2,1)S(1)}, bf16[384,768]{1,0:T(8,128)(2,1)}, u32[]{:S(2)}, u32[]{:S(2)}) collective-permute-start(bf16[384,768]{1,0:T(8,128)(2,1)S(1)} %add_convert_fusion.2), channel_id=1, source_target_pairs={{0,2},{1,3},{2,0},{3,1},{4,6},{5,7},{6,4},{7,5},{8,10},{9,11},{10,... | collective-permute-start | bytes 1769480 | tf_op jit(solution)/shard_map/ppermute | solution.py:151
  113.5 28.5 %collective-permute-start.9 = (bf16[384,768]{1,0:T(8,128)(2,1)S(1)}, bf16[384,768]{1,0:T(8,128)(2,1)}, u32[]{:S(2)}, u32[]{:S(2)}) collective-permute-start(bf16[384,768]{1,0:T(8,128)(2,1)S(1)} %add_convert_fusion.2), channel_id=1, source_target_pairs={{0,1},{1,0},{2,3},{3,2},{4,5},{5,4},{6,7},{7,6},{8,9},{9,8},{10,11... | collective-permute-start | bytes 1769480 | tf_op jit(solution)/shard_map/ppermute | solution.py:151
  115.9 37.2 %collective-permute-start.14 = (bf16[384,768]{1,0:T(8,128)(2,1)}, bf16[384,768]{1,0:T(8,128)(2,1)}, u32[]{:S(2)}, u32[]{:S(2)}) collective-permute-start(bf16[384,768]{1,0:T(8,128)(2,1)} %get-tuple-element.47), channel_id=1, source_target_pairs={{0,3},{1,2},{2,1},{3,0},{4,7},{5,6},{6,5},{7,4},{8,11},{9,10},{10,... | collective-permute-start | bytes 1769480 | tf_op jit(solution)/shard_map/ppermute | solution.py:151
  117.0 49.5 %collective-permute-start.13 = (bf16[384,768]{1,0:T(8,128)(2,1)}, bf16[384,768]{1,0:T(8,128)(2,1)}, u32[]{:S(2)}, u32[]{:S(2)}) collective-permute-start(bf16[384,768]{1,0:T(8,128)(2,1)} %get-tuple-element.47), channel_id=1, source_target_pairs={{0,2},{1,3},{2,0},{3,1},{4,6},{5,7},{6,4},{7,5},{8,10},{9,11},{10,... | collective-permute-start | bytes 1769480 | tf_op jit(solution)/shard_map/ppermute | solution.py:151
  127.8 38.7 %collective-permute-start.12 = (bf16[384,768]{1,0:T(8,128)(2,1)}, bf16[384,768]{1,0:T(8,128)(2,1)S(1)}, u32[]{:S(2)}, u32[]{:S(2)}) collective-permute-start(bf16[384,768]{1,0:T(8,128)(2,1)} %get-tuple-element.47), channel_id=1, source_target_pairs={{0,1},{1,0},{2,3},{3,2},{4,5},{5,4},{6,7},{7,6},{8,9},{9,8},{10,11... | collective-permute-start | bytes 1769480 | tf_op jit(solution)/shard_map/ppermute | solution.py:151
  174.8 27.0 %collective-permute-start.17 = (bf16[384,768]{1,0:T(8,128)(2,1)}, bf16[384,768]{1,0:T(8,128)(2,1)}, u32[]{:S(2)}, u32[]{:S(2)}) collective-permute-start(bf16[384,768]{1,0:T(8,128)(2,1)} %convolution_convert_fusion.7), channel_id=1, source_target_pairs={{0,3},{1,2},{2,1},{3,0},{4,7},{5,6},{6,5},{7,4},{8,11},{9,10},{10,... | collective-permute-start | bytes 1769480 | tf_op jit(solution)/shard_map/ppermute | solution.py:151
  177.5 26.4 %collective-permute-start.16 = (bf16[384,768]{1,0:T(8,128)(2,1)}, bf16[384,768]{1,0:T(8,128)(2,1)}, u32[]{:S(2)}, u32[]{:S(2)}) collective-permute-start(bf16[384,768]{1,0:T(8,128)(2,1)} %convolution_convert_fusion.8), channel_id=1, source_target_pairs={{0,2},{1,3},{2,0},{3,1},{4,6},{5,7},{6,4},{7,5},{8,10},{9,11},{10,... | collective-permute-start | bytes 1769480 | tf_op jit(solution)/shard_map/ppermute | solution.py:151
  179.1 24.8 %collective-permute-start.15 = (bf16[384,768]{1,0:T(8,128)(2,1)}, bf16[384,768]{1,0:T(8,128)(2,1)}, u32[]{:S(2)}, u32[]{:S(2)}) collective-permute-start(bf16[384,768]{1,0:T(8,128)(2,1)} %convolution_convert_fusion.9), channel_id=1, source_target_pairs={{0,1},{1,0},{2,3},{3,2},{4,5},{5,4},{6,7},{7,6},{8,9},{9,8},{10,11... | collective-permute-start | bytes 1769480 | tf_op jit(solution)/shard_map/ppermute | solution.py:151
  200.5 108.0 %collective-permute-start.54 = (bf16[4,96,1536]{2,1,0:T(8,128)(2,1)}, bf16[4,96,1536]{2,1,0:T(8,128)(2,1)}, u32[]{:S(2)}, u32[]{:S(2)}) collective-permute-start(bf16[4,96,1536]{2,1,0:T(8,128)(2,1)} %fusion.9), channel_id=1, source_target_pairs={{0,16},{16,0},{1,17},{17,1},{2,18},{18,2},{3,19},{19,3},{4,20},{20... | collective-permute-start | bytes 3538952 | tf_op jit(solution)/shard_map/ppermute | solution.py:151
  208.7 13.2 %collective-permute-start.48 = (f32[3072]{0:T(1024)S(1)}, f32[3072]{0:T(1024)S(1)}, u32[]{:S(2)}, u32[]{:S(2)}) collective-permute-start(f32[3072]{0:T(1024)S(1)} %pad_maximum_fusion.15), channel_id=1, source_target_pairs={{0,2},{1,3},{2,0},{3,1},{4,6},{5,7},{6,4},{7,5},{8,10},{9,11},{10,... | collective-permute-start | bytes 36872 | tf_op jit(solution)/shard_map/ppermute | solution.py:151
  208.7 13.2 %collective-permute-start.49 = (f32[3072]{0:T(1024)S(1)}, f32[3072]{0:T(1024)S(1)}, u32[]{:S(2)}, u32[]{:S(2)}) collective-permute-start(f32[3072]{0:T(1024)S(1)} %pad_maximum_fusion.15), channel_id=1, source_target_pairs={{0,3},{1,2},{2,1},{3,0},{4,7},{5,6},{6,5},{7,4},{8,11},{9,10},{10,... | collective-permute-start | bytes 36872 | tf_op jit(solution)/shard_map/ppermute | solution.py:151
  209.9 12.0 %collective-permute-start.47 = (f32[3072]{0:T(1024)S(1)}, f32[3072]{0:T(1024)S(1)}, u32[]{:S(2)}, u32[]{:S(2)}) collective-permute-start(f32[3072]{0:T(1024)S(1)} %pad_maximum_fusion.15), channel_id=1, source_target_pairs={{0,1},{1,0},{2,3},{3,2},{4,5},{5,4},{6,7},{7,6},{8,9},{9,8},{10,11... | collective-permute-start | bytes 36872 | tf_op jit(solution)/shard_map/ppermute | solution.py:151
  212.9 80.6 %collective-permute-start.20 = (bf16[384,768]{1,0:T(8,128)(2,1)}, bf16[384,768]{1,0:T(8,128)(2,1)}, u32[]{:S(2)}, u32[]{:S(2)}) collective-permute-start(bf16[384,768]{1,0:T(8,128)(2,1)} %convolution_convert_fusion.4), channel_id=1, source_target_pairs={{0,3},{1,2},{2,1},{3,0},{4,7},{5,6},{6,5},{7,4},{8,11},{9,10},{10,... | collective-permute-start | bytes 1769480 | tf_op jit(solution)/shard_map/ppermute | solution.py:151
  222.4 4.7 %collective-permute-start.52 = (f32[3840]{0:T(1024)S(1)}, f32[3840]{0:T(1024)S(1)}, u32[]{:S(2)}, u32[]{:S(2)}) collective-permute-start(f32[3840]{0:T(1024)S(1)} %pad_maximum_fusion.14), channel_id=1, source_target_pairs={{0,12},{4,8},{8,4},{12,0},{1,13},{5,9},{9,5},{13,1},{2,14},{6,10},... | collective-permute-start | bytes 46088 | tf_op jit(solution)/shard_map/ppermute | solution.py:151
  225.9 7.3 %collective-permute-start.23 = (bf16[384,192]{1,0:T(8,128)(2,1)S(1)}, bf16[384,192]{1,0:T(8,128)(2,1)S(1)}, u32[]{:S(2)}, u32[]{:S(2)}) collective-permute-start(bf16[384,192]{1,0:T(8,128)(2,1)S(1)} %get-tuple-element.67), channel_id=1, source_target_pairs={{0,3},{1,2},{2,1},{3,0},{4,7},{5,6},{6,5},{7,4},{8,11},{9,10},{10,... | collective-permute-start | bytes 442376 | tf_op jit(solution)/shard_map/ppermute | solution.py:151
  227.1 9.9 %collective-permute-start.22 = (bf16[384,192]{1,0:T(8,128)(2,1)S(1)}, bf16[384,192]{1,0:T(8,128)(2,1)S(1)}, u32[]{:S(2)}, u32[]{:S(2)}) collective-permute-start(bf16[384,192]{1,0:T(8,128)(2,1)S(1)} %get-tuple-element.68), channel_id=1, source_target_pairs={{0,2},{1,3},{2,0},{3,1},{4,6},{5,7},{6,4},{7,5},{8,10},{9,11},{10,... | collective-permute-start | bytes 442376 | tf_op jit(solution)/shard_map/ppermute | solution.py:151
  232.3 6.1 %collective-permute-start.21 = (bf16[384,192]{1,0:T(8,128)(2,1)S(1)}, bf16[384,192]{1,0:T(8,128)(2,1)S(1)}, u32[]{:S(2)}, u32[]{:S(2)}) collective-permute-start(bf16[384,192]{1,0:T(8,128)(2,1)S(1)} %get-tuple-element.69), channel_id=1, source_target_pairs={{0,1},{1,0},{2,3},{3,2},{4,5},{5,4},{6,7},{7,6},{8,9},{9,8},{10,11... | collective-permute-start | bytes 442376 | tf_op jit(solution)/shard_map/ppermute | solution.py:151
  233.2 38.4 %collective-permute-start.41 = (bf16[768,192]{0,1:T(8,128)(2,1)S(1)}, bf16[768,192]{0,1:T(8,128)(2,1)S(1)}, u32[]{:S(2)}, u32[]{:S(2)}) collective-permute-start(bf16[768,192]{0,1:T(8,128)(2,1)S(1)} %convolution_convert_fusion.10), channel_id=1, source_target_pairs={{0,3},{1,2},{2,1},{3,0},{4,7},{5,6},{6,5},{7,4},{8,11},{9,10},{10,... | collective-permute-start | bytes 884744 | tf_op jit(solution)/shard_map/ppermute | solution.py:151
  237.1 34.6 %collective-permute-start.40 = (bf16[768,192]{0,1:T(8,128)(2,1)S(1)}, bf16[768,192]{0,1:T(8,128)(2,1)S(1)}, u32[]{:S(2)}, u32[]{:S(2)}) collective-permute-start(bf16[768,192]{0,1:T(8,128)(2,1)S(1)} %convolution_convert_fusion.11), channel_id=1, source_target_pairs={{0,2},{1,3},{2,0},{3,1},{4,6},{5,7},{6,4},{7,5},{8,10},{9,11},{10,... | collective-permute-start | bytes 884744 | tf_op jit(solution)/shard_map/ppermute | solution.py:151
  238.4 33.2 %collective-permute-start.39 = (bf16[768,192]{0,1:T(8,128)(2,1)S(1)}, bf16[768,192]{0,1:T(8,128)(2,1)S(1)}, u32[]{:S(2)}, u32[]{:S(2)}) collective-permute-start(bf16[768,192]{0,1:T(8,128)(2,1)S(1)} %convolution_convert_fusion.12), channel_id=1, source_target_pairs={{0,1},{1,0},{2,3},{3,2},{4,5},{5,4},{6,7},{7,6},{8,9},{9,8},{10,11... | collective-permute-start | bytes 884744 | tf_op jit(solution)/shard_map/ppermute | solution.py:151
  279.5 4.9 %collective-permute-start.45 = (bf16[96,192]{0,1:T(8,128)(2,1)S(1)}, bf16[96,192]{0,1:T(8,128)(2,1)S(1)}, u32[]{:S(2)}, u32[]{:S(2)}) collective-permute-start(bf16[96,192]{0,1:T(8,128)(2,1)S(1)} %get-tuple-element.74), channel_id=1, source_target_pairs={{0,12},{4,8},{8,4},{12,0},{1,13},{5,9},{9,5},{13,1},{2,14},{6,10},... | collective-permute-start | bytes 110600 | tf_op jit(solution)/shard_map/ppermute | solution.py:151
  282.5 5.7 %collective-permute-start.43 = (bf16[96,192]{0,1:T(8,128)(2,1)S(1)}, bf16[96,192]{0,1:T(8,128)(2,1)S(1)}, u32[]{:S(2)}, u32[]{:S(2)}) collective-permute-start(bf16[96,192]{0,1:T(8,128)(2,1)S(1)} %get-tuple-element.73), channel_id=1, source_target_pairs={{0,4},{4,0},{8,12},{12,8},{1,5},{5,1},{9,13},{13,9},{2,6},{6,2},{1... | collective-permute-start | bytes 110600 | tf_op jit(solution)/shard_map/ppermute | solution.py:151
  284.4 13.0 %collective-permute-start.19 = (bf16[384,768]{1,0:T(8,128)(2,1)S(1)}, bf16[384,768]{1,0:T(8,128)(2,1)S(1)}, u32[]{:S(2)}, u32[]{:S(2)}) collective-permute-start(bf16[384,768]{1,0:T(8,128)(2,1)S(1)} %copy-done.43), channel_id=1, source_target_pairs={{0,2},{1,3},{2,0},{3,1},{4,6},{5,7},{6,4},{7,5},{8,10},{9,11},{10,... | collective-permute-start | bytes 1769480 | tf_op jit(solution)/shard_map/ppermute | solution.py:151
  286.9 5.2 %collective-permute-start.34 = (bf16[4,96,576]{2,1,0:T(8,128)(2,1)S(1)}, bf16[4,96,576]{2,1,0:T(8,128)(2,1)S(1)}, u32[]{:S(2)}, u32[]{:S(2)}) collective-permute-start(bf16[4,96,576]{2,1,0:T(8,128)(2,1)S(1)} %fusion.47), channel_id=1, source_target_pairs={{0,16},{16,0},{1,17},{17,1},{2,18},{18,2},{3,19},{19,3},{4,20},{20... | collective-permute-start | bytes 1327112 | tf_op jit(solution)/shard_map/ppermute | solution.py:151
  289.8 14.5 %collective-permute-start.18 = (bf16[384,768]{1,0:T(8,128)(2,1)S(1)}, bf16[384,768]{1,0:T(8,128)(2,1)S(1)}, u32[]{:S(2)}, u32[]{:S(2)}) collective-permute-start(bf16[384,768]{1,0:T(8,128)(2,1)S(1)} %copy-done.42), channel_id=1, source_target_pairs={{0,1},{1,0},{2,3},{3,2},{4,5},{5,4},{6,7},{7,6},{8,9},{9,8},{10,11... | collective-permute-start | bytes 1769480 | tf_op jit(solution)/shard_map/ppermute | solution.py:151
  292.1 28.5 %collective-permute-start.26 = (bf16[384,768]{1,0:T(8,128)(2,1)S(1)}, bf16[384,768]{1,0:T(8,128)(2,1)S(1)}, u32[]{:S(2)}, u32[]{:S(2)}) collective-permute-start(bf16[384,768]{1,0:T(8,128)(2,1)S(1)} %copy-done.45), channel_id=1, source_target_pairs={{0,3},{1,2},{2,1},{3,0},{4,7},{5,6},{6,5},{7,4},{8,11},{9,10},{10,... | collective-permute-start | bytes 1769480 | tf_op jit(solution)/shard_map/ppermute | solution.py:151
  293.5 29.1 %collective-permute-start.25 = (bf16[384,768]{1,0:T(8,128)(2,1)S(1)}, bf16[384,768]{1,0:T(8,128)(2,1)S(1)}, u32[]{:S(2)}, u32[]{:S(2)}) collective-permute-start(bf16[384,768]{1,0:T(8,128)(2,1)S(1)} %copy-done.44), channel_id=1, source_target_pairs={{0,2},{1,3},{2,0},{3,1},{4,6},{5,7},{6,4},{7,5},{8,10},{9,11},{10,... | collective-permute-start | bytes 1769480 | tf_op jit(solution)/shard_map/ppermute | solution.py:151
  297.4 32.4 %collective-permute-start.24 = (bf16[384,768]{1,0:T(8,128)(2,1)S(1)}, bf16[384,768]{1,0:T(8,128)(2,1)S(1)}, u32[]{:S(2)}, u32[]{:S(2)}) collective-permute-start(bf16[384,768]{1,0:T(8,128)(2,1)S(1)} %convolution_convert_fusion.2), channel_id=1, source_target_pairs={{0,1},{1,0},{2,3},{3,2},{4,5},{5,4},{6,7},{7,6},{8,9},{9,8},{10,11... | collective-permute-start | bytes 1769480 | tf_op jit(solution)/shard_map/ppermute | solution.py:151
  304.4 6.0 %collective-permute-start.37 = (bf16[96,576]{1,0:T(8,128)(2,1)S(1)}, bf16[96,576]{1,0:T(8,128)(2,1)S(1)}, u32[]{:S(2)}, u32[]{:S(2)}) collective-permute-start(bf16[96,576]{1,0:T(8,128)(2,1)S(1)} %get-tuple-element.58), channel_id=1, source_target_pairs={{0,12},{4,8},{8,4},{12,0},{1,13},{5,9},{9,5},{13,1},{2,14},{6,10},... | collective-permute-start | bytes 331784 | tf_op jit(solution)/shard_map/ppermute | solution.py:151
  308.5 9.6 %collective-permute-start.36 = (bf16[96,576]{1,0:T(8,128)(2,1)S(1)}, bf16[96,576]{1,0:T(8,128)(2,1)S(1)}, u32[]{:S(2)}, u32[]{:S(2)}) collective-permute-start(bf16[96,576]{1,0:T(8,128)(2,1)S(1)} %get-tuple-element.59), channel_id=1, source_target_pairs={{0,8},{4,12},{8,0},{12,4},{1,9},{5,13},{9,1},{13,5},{2,10},{6,14},... | collective-permute-start | bytes 331784 | tf_op jit(solution)/shard_map/ppermute | solution.py:151
  310.4 9.4 %collective-permute-start.35 = (bf16[96,576]{1,0:T(8,128)(2,1)S(1)}, bf16[96,576]{1,0:T(8,128)(2,1)S(1)}, u32[]{:S(2)}, u32[]{:S(2)}) collective-permute-start(bf16[96,576]{1,0:T(8,128)(2,1)S(1)} %get-tuple-element.57), channel_id=1, source_target_pairs={{0,4},{4,0},{8,12},{12,8},{1,5},{5,1},{9,13},{13,9},{2,6},{6,2},{1... | collective-permute-start | bytes 331784 | tf_op jit(solution)/shard_map/ppermute | solution.py:151
  318.0 33.6 %collective-permute-start.57 = (bf16[96,1536]{1,0:T(8,128)(2,1)}, bf16[96,1536]{1,0:T(8,128)(2,1)}, u32[]{:S(2)}, u32[]{:S(2)}) collective-permute-start(bf16[96,1536]{1,0:T(8,128)(2,1)} %get-tuple-element.52), channel_id=1, source_target_pairs={{0,12},{4,8},{8,4},{12,0},{1,13},{5,9},{9,5},{13,1},{2,14},{6,10},... | collective-permute-start | bytes 884744 | tf_op jit(solution)/shard_map/ppermute | solution.py:151
  319.7 31.9 %collective-permute-start.56 = (bf16[96,1536]{1,0:T(8,128)(2,1)}, bf16[96,1536]{1,0:T(8,128)(2,1)}, u32[]{:S(2)}, u32[]{:S(2)}) collective-permute-start(bf16[96,1536]{1,0:T(8,128)(2,1)} %get-tuple-element.53), channel_id=1, source_target_pairs={{0,8},{4,12},{8,0},{12,4},{1,9},{5,13},{9,1},{13,5},{2,10},{6,14},... | collective-permute-start | bytes 884744 | tf_op jit(solution)/shard_map/ppermute | solution.py:151
  338.5 5.8 %collective-permute-start.31 = (f32[1920]{0:T(1024)S(1)}, f32[1920]{0:T(1024)S(1)}, u32[]{:S(2)}, u32[]{:S(2)}) collective-permute-start(f32[1920]{0:T(1024)S(1)} %concatenate.70), channel_id=1, source_target_pairs={{0,8},{4,12},{8,0},{12,4},{1,9},{5,13},{9,1},{13,5},{2,10},{6,14},... | collective-permute-start | bytes 23048 | tf_op jit(solution)/shard_map/ppermute | solution.py:151
  341.5 6.3 %collective-permute-start.30 = (f32[1920]{0:T(1024)S(1)}, f32[1920]{0:T(1024)S(1)}, u32[]{:S(2)}, u32[]{:S(2)}) collective-permute-start(f32[1920]{0:T(1024)S(1)} %concatenate.70), channel_id=1, source_target_pairs={{0,4},{4,0},{8,12},{12,8},{1,5},{5,1},{9,13},{13,9},{2,6},{6,2},{1... | collective-permute-start | bytes 23048 | tf_op jit(solution)/shard_map/ppermute | solution.py:151
  344.3 7.6 %collective-permute-start.55 = (bf16[96,1536]{1,0:T(8,128)(2,1)}, bf16[96,1536]{1,0:T(8,128)(2,1)S(1)}, u32[]{:S(2)}, u32[]{:S(2)}) collective-permute-start(bf16[96,1536]{1,0:T(8,128)(2,1)} %get-tuple-element.51), channel_id=1, source_target_pairs={{0,4},{4,0},{8,12},{12,8},{1,5},{5,1},{9,13},{13,9},{2,6},{6,2},{1... | collective-permute-start | bytes 884744 | tf_op jit(solution)/shard_map/ppermute | solution.py:151
  344.3 11.7 %collective-permute-start.38 = (f32[96,576]{1,0:T(8,128)}, f32[96,576]{1,0:T(8,128)S(1)}, u32[]{:S(2)}, u32[]{:S(2)}) collective-permute-start(f32[96,576]{1,0:T(8,128)} %fusion.62), channel_id=1, source_target_pairs={{0,16},{16,0},{1,17},{17,1},{2,18},{18,2},{3,19},{19,3},{4,20},{20... | collective-permute-start | bytes 663560 | tf_op jit(solution)/shard_map/ppermute | solution.py:151
  (71 other events, 583.3 us)
Sparse Core Ops, SparseCore 0:
  10.8 69.2 all-gather.1

commit v2 on v1

v2 whole, which is shorter than its diff:
```python
import functools

import jax
import jax.numpy as jnp
from jax import lax
from jax.experimental import pallas as pl
from jax.experimental.pallas import tpu as pltpu
from jax.sharding import PartitionSpec as P

HEAD_DIM = 64
LENGTH = 1500
LOG2E = 1.4426950408889634
SCALE = HEAD_DIM**-0.5
BLOCK = 256
F32 = jnp.float32
BF16 = jnp.bfloat16


def dims(left_dim, right_dim):
    return (((left_dim,), (right_dim,)), ((), ()))


def dot(left_side, right_side, left_dim, right_dim):
    return lax.dot_general(
        left_side, right_side, dims(left_dim, right_dim), preferred_element_type=F32
    )


def norm_stats(stream):
    center = jnp.mean(stream, axis=1, keepdims=True)
    second = jnp.mean(stream * stream, axis=1, keepdims=True)
    inverse = lax.rsqrt(second - center * center + 1e-05)
    return (stream - center) * inverse, inverse


def norm_backward(upstream, normed, inverse, scale_row):
    scaled = upstream * scale_row
    back_rows = inverse * (
        scaled
        - jnp.mean(scaled, axis=1, keepdims=True)
        - normed * jnp.mean(scaled * normed, axis=1, keepdims=True)
    )
    return back_rows, jnp.sum(upstream * normed, axis=0), jnp.sum(upstream, axis=0)


def key_bias(keys, block_rows, real_rows):
    at = lax.broadcasted_iota(jnp.int32, (keys, 1), 0)
    return jnp.where(lax.rem(at, block_rows) < real_rows, 0.0, -1e30).astype(F32)


def head_at(kind, heads, head):
    start = (kind * heads + head) * HEAD_DIM
    return slice(start, start + HEAD_DIM)


def forward_kernel(heads, block_rows, real_rows, part_ref, whole_ref, o_ref, lse_ref):
    bias = key_bias(whole_ref.shape[0], block_rows, real_rows)
    for head in range(heads):
        queries = part_ref[:, head_at(0, heads, head)]
        keys = whole_ref[:, head_at(1, heads, head)]
        values = whole_ref[:, head_at(2, heads, head)]
        scores = dot(keys, queries, 1, 1) * (SCALE * LOG2E) + bias
        highest = jnp.max(scores, axis=0, keepdims=True)
        exponent = jnp.exp2(scores - highest)
        summed = jnp.sum(exponent, axis=0, keepdims=True)
        probs = (exponent * (1.0 / summed)).astype(BF16)
        turned = dot(values, probs, 0, 0)
        o_ref[:, head_at(0, heads, head)] = jnp.transpose(turned).astype(BF16)
        lse_ref[head : head + 1, :] = highest + jnp.log2(summed)


def backward_kernel(
    heads, block_rows, real_rows, part_ref, whole_ref, g_ref, lse_ref, out_ref, dk_sum, dv_sum
):
    step = pl.program_id(0)

    @pl.when(step == 0)
    def _():
        dk_sum[...] = jnp.zeros_like(dk_sum)
        dv_sum[...] = jnp.zeros_like(dv_sum)

    bias = key_bias(whole_ref.shape[0], block_rows, real_rows)
    at = pl.ds(pl.multiple_of(step * BLOCK, BLOCK), BLOCK)
    for head in range(heads):
        queries = part_ref[:, head_at(0, heads, head)]
        keys = whole_ref[:, head_at(1, heads, head)]
        values = whole_ref[:, head_at(2, heads, head)]
        grads = g_ref[:, head_at(0, heads, head)]
        scores = dot(keys, queries, 1, 1) * (SCALE * LOG2E) + bias
        probs = jnp.exp2(scores - lse_ref[head : head + 1, :])
        prob_grad = dot(values, grads, 1, 1)
        inner = jnp.sum(probs * prob_grad, axis=0, keepdims=True)
        score_grad = (probs * (prob_grad - inner)).astype(BF16)
        dv_sum[head] += dot(probs.astype(BF16), grads, 1, 0)
        dk_sum[head] += dot(score_grad, queries, 1, 0)
        turned = dot(keys, score_grad, 0, 0)
        out_ref[at, head_at(0, heads, head)] = (jnp.transpose(turned) * SCALE).astype(BF16)

    @pl.when(step == pl.num_programs(0) - 1)
    def _():
        for head in range(heads):
            out_ref[:, head_at(1, heads, head)] = (dk_sum[head] * SCALE).astype(BF16)
            out_ref[:, head_at(2, heads, head)] = dv_sum[head].astype(BF16)


def attention_forward(qkv, first, count, block_rows, real_rows):
    tokens, width = qkv.shape[0], qkv.shape[1] // 3
    heads = width // HEAD_DIM
    start = first // BLOCK
    return pl.pallas_call(
        functools.partial(forward_kernel, heads, block_rows, real_rows),
        grid=(count // BLOCK,),
        in_specs=[
            pl.BlockSpec((BLOCK, 3 * width), lambda i: (i + start, 0)),
            pl.BlockSpec((tokens, 3 * width), lambda i: (0, 0)),
        ],
        out_specs=[
            pl.BlockSpec((BLOCK, width), lambda i: (i, 0)),
            pl.BlockSpec((8, BLOCK), lambda i: (0, i)),
        ],
        out_shape=[
            jax.ShapeDtypeStruct((count, width), BF16),
            jax.ShapeDtypeStruct((8, count), F32),
        ],
        compiler_params=pltpu.CompilerParams(vmem_limit_bytes=40 * 1024 * 1024),
        cost_estimate=pl.CostEstimate(
            flops=16 * count * tokens * width,
            bytes_accessed=8 * tokens * width,
            transcendentals=heads * count * tokens,
        ),
        name="attention_forward",
    )(qkv, qkv)


def attention_backward(qkv, grads, lse, block_rows, real_rows):
    tokens, width = grads.shape
    heads = width // HEAD_DIM
    whole = pl.BlockSpec((tokens, 3 * width), lambda i: (0, 0))
    return pl.pallas_call(
        functools.partial(backward_kernel, heads, block_rows, real_rows),
        grid=(tokens // BLOCK,),
        in_specs=[
            pl.BlockSpec((BLOCK, 3 * width), lambda i: (i, 0)),
            whole,
            pl.BlockSpec((BLOCK, width), lambda i: (i, 0)),
            pl.BlockSpec((8, BLOCK), lambda i: (0, i)),
        ],
        out_specs=whole,
        out_shape=jax.ShapeDtypeStruct((tokens, 3 * width), BF16),
        scratch_shapes=[
            pltpu.VMEM((heads, tokens, HEAD_DIM), F32),
            pltpu.VMEM((heads, tokens, HEAD_DIM), F32),
        ],
        compiler_params=pltpu.CompilerParams(vmem_limit_bytes=40 * 1024 * 1024),
        cost_estimate=pl.CostEstimate(
            flops=40 * tokens * tokens * width,
            bytes_accessed=14 * tokens * width,
            transcendentals=heads * tokens * tokens,
        ),
        name="attention_backward",
    )(qkv, qkv, grads, lse)


def swap(block, axis, size, step):
    return lax.ppermute(block, axis, [(i, i ^ step) for i in range(size)])


def few(size):
    return size <= 8 and size & (size - 1) == 0


def tree(terms):
    while len(terms) > 1:
        terms = [terms[i] + terms[i + 1] for i in range(0, len(terms), 2)]
    return terms[0]


def spread(block, axis, size):
    return [block] + [swap(block, axis, size, j) for j in range(1, size)]


def exchange(blocks, axis, size):
    return [blocks[0]] + [swap(blocks[j], axis, size, j) for j in range(1, size)]


def gather_rows(block, axis, size):
    if size != 4:
        return jnp.concatenate(spread(block, axis, size), axis=0)
    half = block.shape[1] // 2
    one = swap(block, axis, size, 1)
    two = swap(block, axis, size, 2)
    left = swap(one[:, :half], axis, size, 2)
    right = swap(two[:, half:], axis, size, 1)
    return jnp.concatenate([block, one, two, jnp.concatenate([left, right], axis=1)], axis=0)


def sum_blocks(make, axis, size):
    sent = {j: swap(make(j).astype(BF16), axis, size, j) for j in reversed(range(1, size))}
    return tree([make(0)] + [sent[j].astype(F32) for j in range(1, size)])


def send_products(source, weight, held, axis, size):
    rows = lambda j: source[j * held : (j + 1) * held]
    if size != 4:
        return [swap(dot(rows(j), weight, 1, 1).astype(BF16), axis, size, j) for j in range(1, size)]
    half = weight.shape[0] // 2
    pair = jnp.concatenate([rows(1), rows(3)], axis=0)
    one = swap(dot(pair, weight[:half], 1, 1).astype(BF16), axis, size, 1)
    two = swap(dot(source[2 * held :], weight[half:], 1, 1).astype(BF16), axis, size, 2)
    return [one, two]


def add_products(found, source, weight, held, axis, size):
    rows = lambda j: source[j * held : (j + 1) * held]
    own = dot(rows(0), weight, 1, 1)
    if size != 4:
        return tree([own] + [term.astype(F32) for term in found])
    half = weight.shape[0] // 2
    one, two = found
    far_left = dot(rows(2), weight[:half], 1, 1) + one[held:].astype(F32)
    far_right = dot(rows(1), weight[half:], 1, 1) + two[held:].astype(F32)
    left_back = swap(far_left.astype(BF16), axis, size, 2)
    right_back = swap(far_right.astype(BF16), axis, size, 1)
    near = jnp.concatenate([one[:held], two[:held]], axis=1).astype(F32)
    back = jnp.concatenate([left_back, right_back], axis=1).astype(F32)
    return own + near + back


def sum_products(source, weight, held, axis, size):
    found = send_products(source, weight, held, axis, size)
    return add_products(found, source, weight, held, axis, size)


def sum_all(vector, axis, size):
    if few(size):
        return tree(spread(vector, axis, size))
    return lax.psum(vector, axis)


def gather_weight(block, rows, dps, offload):
    if dps != 2:
        return lax.all_gather(block, "row", axis=0, tiled=True)
    half = block.shape[0] // 2
    first = lax.axis_index("dp") == 0
    mine = jnp.where(first, block[:half], block[half:])
    if offload or not few(rows):
        return lax.all_gather(mine, ("row", "dp"), axis=0, tiled=True)
    me = lax.axis_index("row")
    found = jnp.stack(spread(mine, "row", rows))
    order = [
        lax.dynamic_index_in_dim(found, jnp.bitwise_xor(me, r), 0, False) for r in range(rows)
    ]
    mine = jnp.stack(order)
    theirs = swap(mine, "dp", 2, 1)
    whole = jnp.stack([jnp.where(first, mine, theirs), jnp.where(first, theirs, mine)], axis=1)
    return whole.reshape(2 * half * rows, block.shape[1])


def halve_weight(part, rows, dps):
    depth, width = part.shape
    half = depth // rows // dps
    first = lax.axis_index("dp") == 0
    view = part.reshape(rows, dps, half, width)
    mine = jnp.where(first, view[:, 0], view[:, 1])
    other = jnp.where(first, view[:, 1], view[:, 0]).astype(BF16)
    return mine + swap(other, "dp", dps, 1).astype(F32)


def sum_weight(total, rows):
    if few(rows):
        me = lax.axis_index("row")
        pick = lambda j: lax.dynamic_index_in_dim(total, jnp.bitwise_xor(me, j), 0, False)
        return sum_blocks(pick, "row", rows)
    return lax.psum_scatter(total, "row", scatter_dimension=0, tiled=True)[0]


def rejoin_weight(total, dps):
    first = lax.axis_index("dp") == 0
    theirs = swap(total, "dp", dps, 1)
    return jnp.where(
        first,
        jnp.concatenate([total, theirs], axis=0),
        jnp.concatenate([theirs, total], axis=0),
    )


def per_device(
    cols, rows, dps,
    inputs, first_gain, first_shift, query_weight, query_bias, key_weight, value_weight,
    value_bias, out_weight, out_bias, second_gain, second_shift, up_weight, up_bias,
    down_weight, down_bias, cotangent,
):
    real = inputs.shape[0]
    held = -(-real // 128) * 128
    width = inputs.shape[1]
    head_cols = query_weight.shape[1]
    assert real * cols == LENGTH and cols & (cols - 1) == 0
    fill = ((0, held - real), (0, 0))
    padded = jnp.pad(inputs, fill)
    cotangent = jnp.pad(cotangent, fill)

    def block(array, j):
        return array[j * held : (j + 1) * held]

    def join(blocks):
        return jnp.concatenate(blocks, axis=0)

    assert dps == 2
    first_normed, first_inverse = norm_stats(padded)
    attn_in = (first_normed * first_gain + first_shift).astype(BF16)
    near = gather_weight(
        jnp.concatenate([query_weight, key_weight, value_weight, out_weight.T], axis=1),
        rows, dps, False,
    )
    joined, out_turned = near[:, : 3 * head_cols], near[:, 3 * head_cols :]
    attn_all = gather_rows(attn_in, "col", cols)
    rest = gather_weight(jnp.concatenate([up_weight, down_weight.T], axis=1), rows, dps, True)
    hidden_cols = up_weight.shape[1]
    up_full, down_turned = rest[:, :hidden_cols], rest[:, hidden_cols:]

    joined_bias = jnp.concatenate([query_bias, jnp.zeros_like(query_bias), value_bias])
    qkv = (dot(attn_all, joined, 1, 0) + joined_bias).astype(BF16)

    out_grad = cotangent.astype(BF16)
    out_all = gather_rows(out_grad, "col", cols)
    out_full = jnp.concatenate(spread(out_turned, "col", cols), axis=1)
    middle_at = cols // 2 * held
    attended_far, lse_far = attention_forward(
        qkv, middle_at, cols * held - middle_at, held, real
    )
    qkv, out_all, out_full, up_full, down_turned = lax.optimization_barrier(
        (qkv, out_all, out_full, up_full, down_turned)
    )
    attended_near, lse_near = attention_forward(qkv, 0, middle_at, held, real)
    halves = [block(attended_near, j) for j in range(cols // 2)]
    halves += [block(attended_far, j) for j in range(cols - cols // 2)]
    attended_own = jnp.concatenate(exchange(halves, "col", cols), axis=1)
    lse = jnp.concatenate([lse_near, lse_far], axis=1)

    middle = padded + (dot(attended_own, out_full, 1, 1) + out_bias)
    second_normed, second_inverse = norm_stats(middle)
    mlp_in = (second_normed * second_gain + second_shift).astype(BF16)
    mlp_all = gather_rows(mlp_in, "col", cols)
    pre_act = dot(mlp_all, up_full, 1, 0) + up_bias
    hidden_grad = dot(out_all, down_turned, 1, 0)
    below = 0.5 * (1.0 + lax.erf(pre_act * (0.5**0.5)))
    slope = below + pre_act * (jnp.exp(-0.5 * pre_act * pre_act) * 0.3989422804014327)
    hidden = (pre_act * below).astype(BF16)
    pre_grad = (hidden_grad * slope).astype(BF16)
    mlp_back = sum_products(pre_grad, up_full, held, "col", cols)
    up_part = dot(mlp_all, pre_grad, 0, 0)
    down_part = dot(out_all, hidden, 0, 0)
    mlp_half = halve_weight(jnp.concatenate([up_part, down_part], axis=1), rows, dps)
    up_bias_part = jnp.sum(pre_grad, axis=0, dtype=F32)
    norm_rows, second_gain_part, second_shift_part = norm_backward(
        mlp_back, second_normed, second_inverse, second_gain
    )
    middle_grad = cotangent + norm_rows
    attn_grad = middle_grad.astype(BF16)
    attended_grad_own = dot(attn_grad, out_full, 1, 0).astype(BF16)
    attended_grad = join(
        exchange(
            [attended_grad_own[:, j * head_cols : (j + 1) * head_cols] for j in range(cols)],
            "col",
            cols,
        )
    )

    attended_grad, hidden_late, mlp_half, attn_late = lax.optimization_barrier(
        (attended_grad, hidden, mlp_half, attn_grad)
    )
    down_found = send_products(hidden_late, down_turned, held, "col", cols)
    mlp_sum = sum_weight(mlp_half, rows)
    out_part = sum_blocks(
        lambda j: dot(attn_late, attended_own[:, j * head_cols : (j + 1) * head_cols], 0, 0),
        "col",
        cols,
    )
    grad_rows = attention_backward(qkv, attended_grad, lse, held, real)
    grad_rows, down_found, mlp_sum = lax.optimization_barrier((grad_rows, down_found, mlp_sum))
    down_sum = add_products(down_found, hidden_late, down_turned, held, "col", cols)
    result = middle + (down_sum + down_bias)

    attn_back = sum_products(grad_rows, joined, held, "col", cols)
    near_part = jnp.concatenate([dot(attn_all, grad_rows, 0, 0), out_part], axis=1)
    near_sum = rejoin_weight(sum_weight(halve_weight(near_part, rows, dps), rows), dps)
    mlp_sum = rejoin_weight(mlp_sum, dps)
    qkv_sum, out_sum = near_sum[:, : 3 * head_cols], near_sum[:, 3 * head_cols :]
    norm_rows, first_gain_part, first_shift_part = norm_backward(
        attn_back, first_normed, first_inverse, first_gain
    )
    inputs_grad = middle_grad + norm_rows
    vector = jnp.concatenate([
        first_gain_part,
        first_shift_part,
        second_gain_part,
        second_shift_part,
        jnp.sum(attn_grad, axis=0, dtype=F32),
        jnp.sum(out_grad, axis=0, dtype=F32),
    ])
    row_sums = jnp.sum(grad_rows, axis=0, dtype=F32)
    vector = jnp.concatenate([sum_all(vector, "col", cols), row_sums, up_bias_part])
    vector = sum_all(sum_all(vector, "row", rows), "dp", dps)
    grads = [vector[i * width : (i + 1) * width] for i in range(6)]
    tail = vector[6 * width :]

    return (
        result[:real],
        inputs_grad[:real],
        grads[0],
        grads[1],
        qkv_sum[:, :head_cols],
        tail[:head_cols],
        qkv_sum[:, head_cols : 2 * head_cols],
        qkv_sum[:, 2 * head_cols :],
        tail[2 * head_cols : 3 * head_cols],
        out_sum.T,
        grads[4],
        grads[2],
        grads[3],
        mlp_sum[:, :hidden_cols],
        tail[3 * head_cols :],
        mlp_sum[:, hidden_cols:].T,
        grads[5],
    )


def solution(mesh):
    stream = P(("dp", "row", "col"), None)
    inward, outward = P("row", "col"), P("col", "row")
    return jax.shard_map(
        functools.partial(
            per_device, mesh.shape["col"], mesh.shape["row"], mesh.shape["dp"]
        ),
        mesh=mesh,
        in_specs=(
            stream, P(), P(), inward, P("col"), inward, inward, P("col"), outward, P(), P(), P(),
            inward, P("col"), outward, P(), stream,
        ),
        out_specs=(
            stream, stream, P(), P(), inward, P("col"), inward, inward, P("col"), outward, P(),
            P(), P(), inward, P("col"), outward, P(),
        ),
        check_vma=False,
    )
```

time: 372 us -> 324 us (0.87)
  waiting for transfers between devices: 107 us -> 64.5 us
  blocking collectives: 29.5 us -> 0 us
  starting transfers between devices: 58.7 us -> 87.7 us
  matrix products: 51.8 us -> 44.9 us
  other arithmetic: 25.5 us -> 30.5 us
    ppermute x59 -> x57, waiting for transfers between devices: 105 us -> 64.4 us  [swap(): return lax.ppermute(block, axis, [(i, i ^ step) for i in range(size)])]
    all_gather x1 -> x0, blocking collectives: 29.5 us -> none  [per_device(): lax.all_gather(jnp.concatenate([query_weight, key_weight, value_weight],...]
    ppermute x59 -> x57, starting transfers between devices: 58.7 us -> 87.7 us  [swap(): return lax.ppermute(block, axis, [(i, i ^ step) for i in range(size)])]
    concatenate x5 -> x6, other arithmetic: 0.9 us -> 11.6 us  [the longest x1 8.33 us: gather_rows(): jnp.concatenate([block, one, two, jnp.concatenate([left, right], axis=1)]...]
    dot_general x24 -> x27, matrix products: 51.8 us -> 44.9 us  [dot(): lax.dot_general(left_side, right_side, dims(left_dim, right_dim), preferr...]
    select_n x2 -> x4, other arithmetic: 0.13 us -> 4.88 us  [the longest x2 2.85 us: rejoin_weight(): jnp.where(first, jnp.concatenate([total, theirs], axis=0), jnp.concatenat...]
    unnamed x122 -> x137, local copies, waits for them, and re-layouts: 7.81 us -> 4.77 us
    slice x8 -> x22, local copies, waits for them, and re-layouts: 7.95 us -> 10.4 us  [the longest x1 2.98 us: per_device(): up_full, down_turned = (rest[:, :hidden_cols], rest[:, hidden_cols:])]
  transfers between devices with their start and end apart: 60 -> 58, of which waited for: 26 -> 19; matrix products, arithmetic and copies ran while one was open for 25% -> 23% of each run, Pallas kernels for 13% -> 15%
where the time goes in v2:
time: 324 us; the launch traced here: 318 us
  starting transfers between devices  87.7 us (27%)
  waiting for transfers between devices  64.5 us (20%)
  Pallas kernels  48 us (15%)
  matrix products  44.9 us (14%)
  other arithmetic  30.5 us (9%)
  local copies, waits for them, and re-layouts  27 us (8%)
  between operations  15.7 us (5%)
    ppermute x57, starting transfers between devices, swap(): return lax.ppermute(block, axis, [(i, i ^ step) for i in range(size)])  87.7 us
    ppermute x57, waiting for transfers between devices, swap(): return lax.ppermute(block, axis, [(i, i ^ step) for i in range(size)])  64.4 us
    dot_general x27, matrix products, dot(): lax.dot_general(left_side, right_side, dims(left_dim, right_dim), preferr...  44.9 us
    pallas_call x1, Pallas kernels, attention_backward(): pl.pallas_call(functools.partial(backward_kernel, heads, block_rows, real...  25 us
    pallas_call x2, Pallas kernels, attention_forward(): pl.pallas_call(functools.partial(forward_kernel, heads, block_rows, real_...  23 us
    concatenate x1, other arithmetic, gather_rows(): jnp.concatenate([block, one, two, jnp.concatenate([left, right], axis=1)]...  8.33 us
  transfers between devices with their start and end apart: 58, of which 19 were waited for; matrix products, arithmetic and copies ran while one was open for 23% of the time, Pallas kernels for 15%

profile of v2, /device:TPU:5, one launch (start us, length us, event | category | flops | bytes accessed | tf_op | source)
XLA Modules:
  0.0 318.4 jit_solution(18329760247029128436)
XLA Ops:
  7.3 2.0 fusion.80
  11.0 2.3 collective-permute-start.5
  17.3 5.5 %collective-permute-done.6 = bf16[96,768]{1,0:T(8,128)(2,1)S(1)} collective-permute-done((bf16[96,768]{1,0:T(8,128)(2,1)S(1)}, bf16[96,768]{1,0:T(8,128)(2,1)S(1)}, u32[]{:S(2)}, u32[]{:S(2)}) %collective-permute-start.6) | collective-permute-done | bytes 147488 | tf_op jit(solution)/shard_map/ppermute | solution.py:165
  23.1 8.3 %collective-permute-start.7 = (bf16[4,96,768]{2,1,0:T(8,128)(2,1)S(1)}, bf16[4,96,768]{2,1,0:T(8,128)(2,1)S(1)}, u32[]{:S(2)}, u32[]{:S(2)}) collective-permute-start(bf16[4,96,768]{2,1,0:T(8,128)(2,1)S(1)} %pad_maximum_fusion.6), channel_id=1, source_target_pairs={{0,16},{16,0},{1,17},{17,1},{2,18},{18,2},{3,19},{19,3},{4,20},{20... | collective-permute-start | bytes 1769480 | tf_op jit(solution)/shard_map/ppermute | solution.py:165
  35.1 4.9 %collective-permute-done.8 = bf16[384,768]{1,0:T(8,128)(2,1)S(1)} collective-permute-done((bf16[384,768]{1,0:T(8,128)(2,1)S(1)}, bf16[384,768]{1,0:T(8,128)(2,1)S(1)}, u32[]{:S(2)}, u32[]{:S(2)}) %collective-permute-start.8) | collective-permute-done | bytes 589856 | tf_op jit(solution)/shard_map/ppermute | solution.py:165
  42.7 3.6 %collective-permute-done.2 = bf16[384,384]{1,0:T(8,128)(2,1)S(1)} collective-permute-done((bf16[384,384]{1,0:T(8,128)(2,1)S(1)}, bf16[384,384]{1,0:T(8,128)(2,1)S(1)}, u32[]{:S(2)}, u32[]{:S(2)}) %collective-permute-start.2) | collective-permute-done | bytes 294944 | tf_op jit(solution)/shard_map/ppermute | solution.py:165
  47.6 3.1 add_convert_fusion.part_ref.whole_ref
  50.7 11.6 %attention_forward.3 = (bf16[768,192]{1,0:T(8,128)(2,1)S(1)}, f32[8,768]{1,0:T(8,128)S(1)}) custom-call(bf16[1536,576]{1,0:T(8,128)(2,1)S(1)} %add_convert_fusion.part_ref.whole_ref, bf16[1536,576]{1,0:T(8,128)(2,1)S(1)} %add_convert_fusion.part_ref.whole_ref), custom_call_target="tpu_custom_call" | custom-call | flops 3623878656 | bytes 2359296 | tf_op jit(solution)/shard_map/attention_forward/pallas_call | solution.py:110
  65.0 8.3 %maximum_maximum_fusion.1 = bf16[1536,768]{1,0:T(8,128)(2,1)} fusion(bf16[384,384]{1,0:T(8,128)(2,1)S(1)} %collective-permute-done.11, bf16[384,384]{1,0:T(8,128)(2,1)S(1)} %collective-permute-done.10, bf16[384,768]{1,0:T(8,128)(2,1)S(1)} %collective-permute-done.9, bf16[384,768]{1,0:T(8,128)(2,1)S(1)} %collective-permute-done.8, ...), kind=kLoop, calls=%fused_computation.14 | loop fusion | flops 11796480 | bytes 4718592 | tf_op jit(solution)/shard_map/concatenate | solution.py:194
  74.8 3.0 fusion.101
  77.8 11.4 %attention_forward.2 = (bf16[768,192]{1,0:T(8,128)(2,1)S(1)}, f32[8,768]{1,0:T(8,128)S(1)}) custom-call(bf16[1536,576]{1,0:T(8,128)(2,1)S(1)} %copy-done.1, bf16[1536,576]{1,0:T(8,128)(2,1)S(1)} %copy-done.1), custom_call_target="tpu_custom_call" | custom-call | flops 3623878656 | bytes 2359296 | tf_op jit(solution)/shard_map/attention_forward/pallas_call | solution.py:110
  89.4 4.4 %collective-permute-done.15 = bf16[384,192]{1,0:T(8,128)(2,1)S(1)} collective-permute-done((bf16[384,192]{1,0:T(8,128)(2,1)S(1)}, bf16[384,192]{1,0:T(8,128)(2,1)S(1)}, u32[]{:S(2)}, u32[]{:S(2)}) %collective-permute-start.15) | collective-permute-done | bytes 147488 | tf_op jit(solution)/shard_map/ppermute | solution.py:165
  96.5 9.5 %collective-permute-done.18 = bf16[384,768]{1,0:T(8,128)(2,1)S(1)} collective-permute-done((bf16[384,768]{1,0:T(8,128)(2,1)S(1)}, bf16[384,768]{1,0:T(8,128)(2,1)S(1)}, u32[]{:S(2)}, u32[]{:S(2)}) %collective-permute-start.18) | collective-permute-done | bytes 589856 | tf_op jit(solution)/shard_map/ppermute | solution.py:165
  109.1 5.5 %collective-permute-done.20 = bf16[384,384]{1,0:T(8,128)(2,1)} collective-permute-done((bf16[384,384]{1,0:T(8,128)(2,1)}, bf16[384,384]{1,0:T(8,128)(2,1)}, u32[]{:S(2)}, u32[]{:S(2)}) %collective-permute-start.20) | collective-permute-done | bytes 294944 | tf_op jit(solution)/shard_map/ppermute | solution.py:165
  114.6 2.6 collective-permute-done.21
  117.2 5.5 %multiply_convert_fusion = (bf16[1536,768]{1,0:T(8,128)(2,1)S(1)}, f32[1536,768]{1,0:T(8,128)S(1)}) fusion(f32[768]{0:T(1024)S(1)} %copy-done.64, bf16[768,768]{1,0:T(8,128)(2,1)} %get-tuple-element.40, bf16[384,384]{1,0:T(8,128)(2,1)} %collective-permute-done.21, bf16[384,384]{1,0:T(8,128)(2,1)} %collective-permute-done.20, ...), kind=kOutput, calls=%fused_computation.9 | convolution fusion | flops 1830813696 | bytes 10619904 | tf_op jit(solution)/shard_map/dot_general | solution.py:24
  122.7 4.0 %convert_reduce_fusion = (f32[768]{0:T(1024)}, bf16[1536,768]{1,0:T(8,128)(2,1)S(1)}) fusion(f32[1536,768]{1,0:T(8,128)S(1)} %get-tuple-element.157, f32[768]{0:T(1024)S(1)} %copy-done.64, bf16[1536,768]{1,0:T(8,128)(2,1)S(1)} %copy-done.14, bf16[768,768]{1,0:T(8,128)(2,1)S(1)} %get-tuple-element.39), kind=kOutput, calls=%fused_computation.8 | convolution fusion | flops 1827273984 | bytes 10622976 | tf_op jit(solution)/shard_map/dot_general | solution.py:24
  126.8 2.0 copy-done.21
  133.5 3.2 %fusion.94 = f32[768,768]{0,1:T(8,128)S(1)} fusion(bf16[1536,768]{1,0:T(8,128)(2,1)S(1)} %get-tuple-element.159, bf16[384,384]{1,0:T(8,128)(2,1)} %collective-permute-done.21, bf16[384,384]{1,0:T(8,128)(2,1)} %collective-permute-done.20, bf16[384,768]{1,0:T(8,128)(2,1)S(1)} %copy-done.42, bf16[384,768]{1,0:T(8,128)(2,1)S(1)} %copy-done.40, ...), kind=kOutput, calls=%fused_computation.189 | convolution fusion | flops 1823735808 | bytes 7077888 | tf_op jit(solution)/shard_map/dot_general | solution.py:24
  136.8 2.1 fusion.108
  138.9 2.5 pad_maximum_fusion
  141.4 6.3 %copy.48 = f32[768,1536]{1,0:T(8,128)} copy(f32[768,1536]{0,1:T(8,128)} %pad_maximum_fusion) | data formatting | bytes 9437184 | tf_op jit(solution)/shard_map/concatenate | solution.py:353
  147.7 2.0 add_convert_fusion.6
  151.0 1.8 add_convert_fusion.5
  153.5 12.9 %collective-permute-start.29 = (bf16[4,96,1536]{2,1,0:T(8,128)(2,1)S(1)}, bf16[4,96,1536]{2,1,0:T(8,128)(2,1)S(1)}, u32[]{:S(2)}, u32[]{:S(2)}) collective-permute-start(bf16[4,96,1536]{2,1,0:T(8,128)(2,1)S(1)} %fusion.12), channel_id=1, source_target_pairs={{0,16},{16,0},{1,17},{17,1},{2,18},{18,2},{3,19},{19,3},{4,20},{20... | collective-permute-start | bytes 3538952 | tf_op jit(solution)/shard_map/ppermute | solution.py:165
  168.4 2.8 multiply_reduce_fusion
  176.2 1.9 collective-permute-done.26
  178.1 3.2 collective-permute-done.27
  184.2 1.7 fusion.50
  186.1 5.3 %collective-permute-start.33 = (bf16[96,1536]{1,0:T(8,128)(2,1)S(1)}, bf16[96,1536]{1,0:T(8,128)(2,1)S(1)}, u32[]{:S(2)}, u32[]{:S(2)}) collective-permute-start(bf16[96,1536]{1,0:T(8,128)(2,1)S(1)} %get-tuple-element.106), channel_id=1, source_target_pairs={{0,8},{4,12},{8,0},{12,4},{1,9},{5,13},{9,1},{13,5},{2,10},{6,14},... | collective-permute-start | bytes 884744 | tf_op jit(solution)/shard_map/ppermute | solution.py:165
  195.3 25.0 %attention_backward.1 = bf16[1536,576]{1,0:T(8,128)(2,1)S(1)} custom-call(bf16[1536,576]{1,0:T(8,128)(2,1)S(1)} %copy-done.2, bf16[1536,576]{1,0:T(8,128)(2,1)S(1)} %copy-done.2, bf16[1536,192]{1,0:T(8,128)(2,1)S(1)} %pad_maximum_fusion.4.g_ref, f32[8,1536]{1,0:T(8,128)S(1)} %pad_maximum_fusion.11.lse_ref), custom_call_target="tpu_custom_call" | custom-call | flops 18119393280 | bytes 4128768 | tf_op jit(solution)/shard_map/attention_backward/pallas_call | solution.py:139
  224.0 4.3 %collective-permute-done.34 = bf16[96,1536]{1,0:T(8,128)(2,1)S(1)} collective-permute-done((bf16[96,1536]{1,0:T(8,128)(2,1)S(1)}, bf16[96,1536]{1,0:T(8,128)(2,1)S(1)}, u32[]{:S(2)}, u32[]{:S(2)}) %collective-permute-start.34) | collective-permute-done | bytes 294944 | tf_op jit(solution)/shard_map/ppermute | solution.py:165
  229.3 2.7 collective-permute-done.31
  235.9 6.5 %collective-permute-start.56 = (f32[96,1536]{1,0:T(8,128)}, f32[96,1536]{1,0:T(8,128)}, u32[]{:S(2)}, u32[]{:S(2)}) collective-permute-start(f32[96,1536]{1,0:T(8,128)} %fusion.45), channel_id=1, source_target_pairs={{0,16},{16,0},{1,17},{17,1},{2,18},{18,2},{3,19},{19,3},{4,20},{20... | collective-permute-start | bytes 1769480 | tf_op jit(solution)/shard_map/ppermute | solution.py:165
  242.4 2.7 fusion.96
  246.7 3.0 copy.53
  249.7 1.9 fusion.33
  253.7 1.8 convolution_convert_fusion.1
  257.2 3.1 collective-permute-done.35
  263.4 2.7 collective-permute-start.53
  266.1 7.8 %collective-permute-done.37 = bf16[768,384]{1,0:T(8,128)(2,1)S(1)} collective-permute-done((bf16[768,384]{1,0:T(8,128)(2,1)S(1)}, bf16[768,384]{1,0:T(8,128)(2,1)S(1)}, u32[]{:S(2)}, u32[]{:S(2)}) %collective-permute-start.37) | collective-permute-done | bytes 589856 | tf_op jit(solution)/shard_map/ppermute | solution.py:165
  273.9 2.5 collective-permute-start.54
  279.1 1.7 maximum_select_fusion
  282.1 2.4 collective-permute-start.55
  284.6 2.4 fusion.97
  293.2 2.7 collective-permute-start.46
  297.7 6.5 %collective-permute-start.47 = (f32[5952]{0:T(1024)S(1)}, f32[5952]{0:T(1024)S(1)}, u32[]{:S(2)}, u32[]{:S(2)}) collective-permute-start(f32[5952]{0:T(1024)S(1)} %add_add_fusion.1), channel_id=1, source_target_pairs={{0,16},{16,0},{1,17},{17,1},{2,18},{18,2},{3,19},{19,3},{4,20},{20... | collective-permute-start | bytes 71432 | tf_op jit(solution)/shard_map/ppermute | solution.py:165
  304.1 2.9 slice_add_fusion
  (312 shorter events, 76.7 us)
Async XLA Ops:
  7.2 67.6 %all-gather.2.cloned.1.call-start = ((), (), s32[]{:S(2)}) async-start(), calls=%async_computation | async-start | bytes 2654208 | tf_op jit(solution)/shard_map/all_gather | solution.py:247
  11.0 6.0 %collective-permute-start.5 = (bf16[96,768]{1,0:T(8,128)(2,1)S(1)}, bf16[96,768]{1,0:T(8,128)(2,1)S(1)}, u32[]{:S(2)}, u32[]{:S(2)}) collective-permute-start(bf16[96,768]{1,0:T(8,128)(2,1)S(1)} %slice_select_fusion), channel_id=1, source_target_pairs={{0,8},{4,12},{8,0},{12,4},{1,9},{5,13},{9,1},{13,5},{2,10},{6,14},... | collective-permute-start | bytes 442376 | tf_op jit(solution)/shard_map/ppermute | solution.py:165
  13.3 9.5 %collective-permute-start.6 = (bf16[96,768]{1,0:T(8,128)(2,1)S(1)}, bf16[96,768]{1,0:T(8,128)(2,1)S(1)}, u32[]{:S(2)}, u32[]{:S(2)}) collective-permute-start(bf16[96,768]{1,0:T(8,128)(2,1)S(1)} %slice_select_fusion), channel_id=1, source_target_pairs={{0,12},{4,8},{8,4},{12,0},{1,13},{5,9},{9,5},{13,1},{2,14},{6,10},... | collective-permute-start | bytes 442376 | tf_op jit(solution)/shard_map/ppermute | solution.py:165
  13.9 17.6 %collective-permute-start = (bf16[384,768]{1,0:T(8,128)(2,1)S(1)}, bf16[384,768]{1,0:T(8,128)(2,1)S(1)}, u32[]{:S(2)}, u32[]{:S(2)}) collective-permute-start(bf16[384,768]{1,0:T(8,128)(2,1)S(1)} %add_convert_fusion.2), channel_id=1, source_target_pairs={{0,1},{1,0},{2,3},{3,2},{4,5},{5,4},{6,7},{7,6},{8,9},{9,8},{10,11... | collective-permute-start | bytes 1769480 | tf_op jit(solution)/shard_map/ppermute | solution.py:165
  15.2 17.7 %collective-permute-start.1 = (bf16[384,768]{1,0:T(8,128)(2,1)S(1)}, bf16[384,768]{1,0:T(8,128)(2,1)}, u32[]{:S(2)}, u32[]{:S(2)}) collective-permute-start(bf16[384,768]{1,0:T(8,128)(2,1)S(1)} %add_convert_fusion.2), channel_id=1, source_target_pairs={{0,2},{1,3},{2,0},{3,1},{4,6},{5,7},{6,4},{7,5},{8,10},{9,11},{10,... | collective-permute-start | bytes 1769480 | tf_op jit(solution)/shard_map/ppermute | solution.py:165
  15.6 24.5 %collective-permute-start.8 = (bf16[384,768]{1,0:T(8,128)(2,1)S(1)}, bf16[384,768]{1,0:T(8,128)(2,1)S(1)}, u32[]{:S(2)}, u32[]{:S(2)}) collective-permute-start(bf16[384,768]{1,0:T(8,128)(2,1)S(1)} %get-tuple-element.98), channel_id=1, source_target_pairs={{0,1},{1,0},{2,3},{3,2},{4,5},{5,4},{6,7},{7,6},{8,9},{9,8},{10,11... | collective-permute-start | bytes 1769480 | tf_op jit(solution)/shard_map/ppermute | solution.py:165
  17.1 23.5 %collective-permute-start.9 = (bf16[384,768]{1,0:T(8,128)(2,1)S(1)}, bf16[384,768]{1,0:T(8,128)(2,1)S(1)}, u32[]{:S(2)}, u32[]{:S(2)}) collective-permute-start(bf16[384,768]{1,0:T(8,128)(2,1)S(1)} %get-tuple-element.98), channel_id=1, source_target_pairs={{0,2},{1,3},{2,0},{3,1},{4,6},{5,7},{6,4},{7,5},{8,10},{9,11},{10,... | collective-permute-start | bytes 1769480 | tf_op jit(solution)/shard_map/ppermute | solution.py:165
  23.1 18.6 %collective-permute-start.7 = (bf16[4,96,768]{2,1,0:T(8,128)(2,1)S(1)}, bf16[4,96,768]{2,1,0:T(8,128)(2,1)S(1)}, u32[]{:S(2)}, u32[]{:S(2)}) collective-permute-start(bf16[4,96,768]{2,1,0:T(8,128)(2,1)S(1)} %pad_maximum_fusion.6), channel_id=1, source_target_pairs={{0,16},{16,0},{1,17},{17,1},{2,18},{18,2},{3,19},{19,3},{4,20},{20... | collective-permute-start | bytes 1769480 | tf_op jit(solution)/shard_map/ppermute | solution.py:165
  31.6 14.7 %collective-permute-start.2 = (bf16[384,384]{1,0:T(8,128)(2,1)S(1)}, bf16[384,384]{1,0:T(8,128)(2,1)S(1)}, u32[]{:S(2)}, u32[]{:S(2)}) collective-permute-start(bf16[384,384]{1,0:T(8,128)(2,1)S(1)} %slice.327), channel_id=1, source_target_pairs={{0,2},{1,3},{2,0},{3,1},{4,6},{5,7},{6,4},{7,5},{8,10},{9,11},{10,... | collective-permute-start | bytes 884744 | tf_op jit(solution)/shard_map/ppermute | solution.py:165
  33.8 12.6 %collective-permute-start.3 = (bf16[384,384]{1,0:T(8,128)(2,1)S(1)}, bf16[384,384]{1,0:T(8,128)(2,1)S(1)}, u32[]{:S(2)}, u32[]{:S(2)}) collective-permute-start(bf16[384,384]{1,0:T(8,128)(2,1)S(1)} %slice.328), channel_id=1, source_target_pairs={{0,1},{1,0},{2,3},{3,2},{4,5},{5,4},{6,7},{7,6},{8,9},{9,8},{10,11... | collective-permute-start | bytes 884744 | tf_op jit(solution)/shard_map/ppermute | solution.py:165
  40.1 22.2 %collective-permute-start.10 = (bf16[384,384]{1,0:T(8,128)(2,1)S(1)}, bf16[384,384]{1,0:T(8,128)(2,1)S(1)}, u32[]{:S(2)}, u32[]{:S(2)}) collective-permute-start(bf16[384,384]{1,0:T(8,128)(2,1)S(1)} %slice.332), channel_id=1, source_target_pairs={{0,2},{1,3},{2,0},{3,1},{4,6},{5,7},{6,4},{7,5},{8,10},{9,11},{10,... | collective-permute-start | bytes 884744 | tf_op jit(solution)/shard_map/ppermute | solution.py:165
  40.7 23.0 %collective-permute-start.11 = (bf16[384,384]{1,0:T(8,128)(2,1)S(1)}, bf16[384,384]{1,0:T(8,128)(2,1)S(1)}, u32[]{:S(2)}, u32[]{:S(2)}) collective-permute-start(bf16[384,384]{1,0:T(8,128)(2,1)S(1)} %slice.333), channel_id=1, source_target_pairs={{0,1},{1,0},{2,3},{3,2},{4,5},{5,4},{6,7},{7,6},{8,9},{9,8},{10,11... | collective-permute-start | bytes 884744 | tf_op jit(solution)/shard_map/ppermute | solution.py:165
  42.2 31.2 %collective-permute-start.12 = (bf16[768,192]{1,0:T(8,128)(2,1)S(1)}, bf16[768,192]{1,0:T(8,128)(2,1)S(1)}, u32[]{:S(2)}, u32[]{:S(2)}) collective-permute-start(bf16[768,192]{1,0:T(8,128)(2,1)S(1)} %slice.334), channel_id=1, source_target_pairs={{0,1},{1,0},{2,3},{3,2},{4,5},{5,4},{6,7},{7,6},{8,9},{9,8},{10,11... | collective-permute-start | bytes 884744 | tf_op jit(solution)/shard_map/ppermute | solution.py:165
  46.3 27.0 %collective-permute-start.13 = (bf16[768,192]{1,0:T(8,128)(2,1)S(1)}, bf16[768,192]{1,0:T(8,128)(2,1)S(1)}, u32[]{:S(2)}, u32[]{:S(2)}) collective-permute-start(bf16[768,192]{1,0:T(8,128)(2,1)S(1)} %slice.334), channel_id=1, source_target_pairs={{0,2},{1,3},{2,0},{3,1},{4,6},{5,7},{6,4},{7,5},{8,10},{9,11},{10,... | collective-permute-start | bytes 884744 | tf_op jit(solution)/shard_map/ppermute | solution.py:165
  46.5 26.8 %collective-permute-start.14 = (bf16[768,192]{1,0:T(8,128)(2,1)S(1)}, bf16[768,192]{1,0:T(8,128)(2,1)S(1)}, u32[]{:S(2)}, u32[]{:S(2)}) collective-permute-start(bf16[768,192]{1,0:T(8,128)(2,1)S(1)} %slice.334), channel_id=1, source_target_pairs={{0,3},{1,2},{2,1},{3,0},{4,7},{5,6},{6,5},{7,4},{8,11},{9,10},{10,... | collective-permute-start | bytes 884744 | tf_op jit(solution)/shard_map/ppermute | solution.py:165
  62.3 27.1 %collective-permute-start.16 = (bf16[384,192]{1,0:T(8,128)(2,1)S(1)}, bf16[384,192]{1,0:T(8,128)(2,1)S(1)}, u32[]{:S(2)}, u32[]{:S(2)}) collective-permute-start(bf16[384,192]{1,0:T(8,128)(2,1)S(1)} %get-tuple-element.140), channel_id=1, source_target_pairs={{0,2},{1,3},{2,0},{3,1},{4,6},{5,7},{6,4},{7,5},{8,10},{9,11},{10,... | collective-permute-start | bytes 442376 | tf_op jit(solution)/shard_map/ppermute | solution.py:165
  63.7 25.8 %collective-permute-start.17 = (bf16[384,192]{1,0:T(8,128)(2,1)S(1)}, bf16[384,192]{1,0:T(8,128)(2,1)S(1)}, u32[]{:S(2)}, u32[]{:S(2)}) collective-permute-start(bf16[384,192]{1,0:T(8,128)(2,1)S(1)} %get-tuple-element.141), channel_id=1, source_target_pairs={{0,3},{1,2},{2,1},{3,0},{4,7},{5,6},{6,5},{7,4},{8,11},{9,10},{10,... | collective-permute-start | bytes 442376 | tf_op jit(solution)/shard_map/ppermute | solution.py:165
  95.1 10.9 %collective-permute-start.18 = (bf16[384,768]{1,0:T(8,128)(2,1)S(1)}, bf16[384,768]{1,0:T(8,128)(2,1)S(1)}, u32[]{:S(2)}, u32[]{:S(2)}) collective-permute-start(bf16[384,768]{1,0:T(8,128)(2,1)S(1)} %add_convert_fusion.1), channel_id=1, source_target_pairs={{0,1},{1,0},{2,3},{3,2},{4,5},{5,4},{6,7},{7,6},{8,9},{9,8},{10,11... | collective-permute-start | bytes 1769480 | tf_op jit(solution)/shard_map/ppermute | solution.py:165
  95.2 11.8 %collective-permute-start.19 = (bf16[384,768]{1,0:T(8,128)(2,1)S(1)}, bf16[384,768]{1,0:T(8,128)(2,1)S(1)}, u32[]{:S(2)}, u32[]{:S(2)}) collective-permute-start(bf16[384,768]{1,0:T(8,128)(2,1)S(1)} %add_convert_fusion.1), channel_id=1, source_target_pairs={{0,2},{1,3},{2,0},{3,1},{4,6},{5,7},{6,4},{7,5},{8,10},{9,11},{10,... | collective-permute-start | bytes 1769480 | tf_op jit(solution)/shard_map/ppermute | solution.py:165
  106.8 7.8 %collective-permute-start.20 = (bf16[384,384]{1,0:T(8,128)(2,1)}, bf16[384,384]{1,0:T(8,128)(2,1)}, u32[]{:S(2)}, u32[]{:S(2)}) collective-permute-start(bf16[384,384]{1,0:T(8,128)(2,1)} %slice.339), channel_id=1, source_target_pairs={{0,2},{1,3},{2,0},{3,1},{4,6},{5,7},{6,4},{7,5},{8,10},{9,11},{10,... | collective-permute-start | bytes 884744 | tf_op jit(solution)/shard_map/ppermute | solution.py:165
  107.9 9.3 %collective-permute-start.21 = (bf16[384,384]{1,0:T(8,128)(2,1)}, bf16[384,384]{1,0:T(8,128)(2,1)}, u32[]{:S(2)}, u32[]{:S(2)}) collective-permute-start(bf16[384,384]{1,0:T(8,128)(2,1)} %slice.340), channel_id=1, source_target_pairs={{0,1},{1,0},{2,3},{3,2},{4,5},{5,4},{6,7},{7,6},{8,9},{9,8},{10,11... | collective-permute-start | bytes 884744 | tf_op jit(solution)/shard_map/ppermute | solution.py:165
  132.2 15.5 %collective-permute-start.22 = (bf16[768,384]{1,0:T(8,128)(2,1)}, bf16[768,384]{1,0:T(8,128)(2,1)}, u32[]{:S(2)}, u32[]{:S(2)}) collective-permute-start(bf16[768,384]{1,0:T(8,128)(2,1)} %convolution_convert_fusion.6), channel_id=1, source_target_pairs={{0,1},{1,0},{2,3},{3,2},{4,5},{5,4},{6,7},{7,6},{8,9},{9,8},{10,11... | collective-permute-start | bytes 1769480 | tf_op jit(solution)/shard_map/ppermute | solution.py:165
  133.3 17.7 %collective-permute-start.23 = (bf16[768,384]{1,0:T(8,128)(2,1)}, bf16[768,384]{1,0:T(8,128)(2,1)}, u32[]{:S(2)}, u32[]{:S(2)}) collective-permute-start(bf16[768,384]{1,0:T(8,128)(2,1)} %convolution_convert_fusion.5), channel_id=1, source_target_pairs={{0,2},{1,3},{2,0},{3,1},{4,6},{5,7},{6,4},{7,5},{8,10},{9,11},{10,... | collective-permute-start | bytes 1769480 | tf_op jit(solution)/shard_map/ppermute | solution.py:165
  149.7 18.6 %collective-permute-start.24 = (bf16[384,384]{1,0:T(8,128)(2,1)S(1)}, bf16[384,384]{1,0:T(8,128)(2,1)S(1)}, u32[]{:S(2)}, u32[]{:S(2)}) collective-permute-start(bf16[384,384]{1,0:T(8,128)(2,1)S(1)} %add_convert_fusion.6), channel_id=1, source_target_pairs={{0,2},{1,3},{2,0},{3,1},{4,6},{5,7},{6,4},{7,5},{8,10},{9,11},{10,... | collective-permute-start | bytes 884744 | tf_op jit(solution)/shard_map/ppermute | solution.py:165
  152.8 15.5 %collective-permute-start.25 = (bf16[384,384]{1,0:T(8,128)(2,1)S(1)}, bf16[384,384]{1,0:T(8,128)(2,1)S(1)}, u32[]{:S(2)}, u32[]{:S(2)}) collective-permute-start(bf16[384,384]{1,0:T(8,128)(2,1)S(1)} %add_convert_fusion.5), channel_id=1, source_target_pairs={{0,1},{1,0},{2,3},{3,2},{4,5},{5,4},{6,7},{7,6},{8,9},{9,8},{10,11... | collective-permute-start | bytes 884744 | tf_op jit(solution)/shard_map/ppermute | solution.py:165
  153.5 28.2 %collective-permute-start.29 = (bf16[4,96,1536]{2,1,0:T(8,128)(2,1)S(1)}, bf16[4,96,1536]{2,1,0:T(8,128)(2,1)S(1)}, u32[]{:S(2)}, u32[]{:S(2)}) collective-permute-start(bf16[4,96,1536]{2,1,0:T(8,128)(2,1)S(1)} %fusion.12), channel_id=1, source_target_pairs={{0,16},{16,0},{1,17},{17,1},{2,18},{18,2},{3,19},{19,3},{4,20},{20... | collective-permute-start | bytes 3538952 | tf_op jit(solution)/shard_map/ppermute | solution.py:165
  174.7 6.5 %collective-permute-start.27 = (bf16[384,192]{1,0:T(8,128)(2,1)S(1)}, bf16[384,192]{1,0:T(8,128)(2,1)S(1)}, u32[]{:S(2)}, u32[]{:S(2)}) collective-permute-start(bf16[384,192]{1,0:T(8,128)(2,1)S(1)} %get-tuple-element.132), channel_id=1, source_target_pairs={{0,2},{1,3},{2,0},{3,1},{4,6},{5,7},{6,4},{7,5},{8,10},{9,11},{10,... | collective-permute-start | bytes 442376 | tf_op jit(solution)/shard_map/ppermute | solution.py:165
  186.0 38.0 %collective-permute-start.32 = (bf16[96,1536]{1,0:T(8,128)(2,1)S(1)}, bf16[96,1536]{1,0:T(8,128)(2,1)S(1)}, u32[]{:S(2)}, u32[]{:S(2)}) collective-permute-start(bf16[96,1536]{1,0:T(8,128)(2,1)S(1)} %get-tuple-element.104), channel_id=1, source_target_pairs={{0,4},{4,0},{8,12},{12,8},{1,5},{5,1},{9,13},{13,9},{2,6},{6,2},{1... | collective-permute-start | bytes 884744 | tf_op jit(solution)/shard_map/ppermute | solution.py:165
  186.1 37.9 %collective-permute-start.33 = (bf16[96,1536]{1,0:T(8,128)(2,1)S(1)}, bf16[96,1536]{1,0:T(8,128)(2,1)S(1)}, u32[]{:S(2)}, u32[]{:S(2)}) collective-permute-start(bf16[96,1536]{1,0:T(8,128)(2,1)S(1)} %get-tuple-element.106), channel_id=1, source_target_pairs={{0,8},{4,12},{8,0},{12,4},{1,9},{5,13},{9,1},{13,5},{2,10},{6,14},... | collective-permute-start | bytes 884744 | tf_op jit(solution)/shard_map/ppermute | solution.py:165
  191.8 29.0 %collective-permute-start.48 = (bf16[768,192]{0,1:T(8,128)(2,1)S(1)}, bf16[768,192]{0,1:T(8,128)(2,1)S(1)}, u32[]{:S(2)}, u32[]{:S(2)}) collective-permute-start(bf16[768,192]{0,1:T(8,128)(2,1)S(1)} %convolution_convert_fusion.9), channel_id=1, source_target_pairs={{0,1},{1,0},{2,3},{3,2},{4,5},{5,4},{6,7},{7,6},{8,9},{9,8},{10,11... | collective-permute-start | bytes 884744 | tf_op jit(solution)/shard_map/ppermute | solution.py:165
  192.2 30.3 %collective-permute-start.49 = (bf16[768,192]{0,1:T(8,128)(2,1)S(1)}, bf16[768,192]{0,1:T(8,128)(2,1)S(1)}, u32[]{:S(2)}, u32[]{:S(2)}) collective-permute-start(bf16[768,192]{0,1:T(8,128)(2,1)S(1)} %convolution_convert_fusion.8), channel_id=1, source_target_pairs={{0,2},{1,3},{2,0},{3,1},{4,6},{5,7},{6,4},{7,5},{8,10},{9,11},{10,... | collective-permute-start | bytes 884744 | tf_op jit(solution)/shard_map/ppermute | solution.py:165
  193.9 28.7 %collective-permute-start.50 = (bf16[768,192]{0,1:T(8,128)(2,1)S(1)}, bf16[768,192]{0,1:T(8,128)(2,1)S(1)}, u32[]{:S(2)}, u32[]{:S(2)}) collective-permute-start(bf16[768,192]{0,1:T(8,128)(2,1)S(1)} %convolution_convert_fusion.7), channel_id=1, source_target_pairs={{0,3},{1,2},{2,1},{3,0},{4,7},{5,6},{6,5},{7,4},{8,11},{9,10},{10,... | collective-permute-start | bytes 884744 | tf_op jit(solution)/shard_map/ppermute | solution.py:165
  220.8 7.5 %collective-permute-start.34 = (bf16[96,1536]{1,0:T(8,128)(2,1)S(1)}, bf16[96,1536]{1,0:T(8,128)(2,1)S(1)}, u32[]{:S(2)}, u32[]{:S(2)}) collective-permute-start(bf16[96,1536]{1,0:T(8,128)(2,1)S(1)} %get-tuple-element.105), channel_id=1, source_target_pairs={{0,12},{4,8},{8,4},{12,0},{1,13},{5,9},{9,5},{13,1},{2,14},{6,10},... | collective-permute-start | bytes 884744 | tf_op jit(solution)/shard_map/ppermute | solution.py:165
  222.5 9.5 %collective-permute-start.31 = (bf16[768,384]{1,0:T(8,128)(2,1)S(1)}, bf16[768,384]{1,0:T(8,128)(2,1)S(1)}, u32[]{:S(2)}, u32[]{:S(2)}) collective-permute-start(bf16[768,384]{1,0:T(8,128)(2,1)S(1)} %convolution_convert_fusion.2), channel_id=1, source_target_pairs={{0,2},{1,3},{2,0},{3,1},{4,6},{5,7},{6,4},{7,5},{8,10},{9,11},{10,... | collective-permute-start | bytes 1769480 | tf_op jit(solution)/shard_map/ppermute | solution.py:165
  222.6 9.4 %collective-permute-start.30 = (bf16[768,384]{1,0:T(8,128)(2,1)S(1)}, bf16[768,384]{1,0:T(8,128)(2,1)S(1)}, u32[]{:S(2)}, u32[]{:S(2)}) collective-permute-start(bf16[768,384]{1,0:T(8,128)(2,1)S(1)} %convolution_convert_fusion.3), channel_id=1, source_target_pairs={{0,1},{1,0},{2,3},{3,2},{4,5},{5,4},{6,7},{7,6},{8,9},{9,8},{10,11... | collective-permute-start | bytes 1769480 | tf_op jit(solution)/shard_map/ppermute | solution.py:165
  235.9 41.8 %collective-permute-start.56 = (f32[96,1536]{1,0:T(8,128)}, f32[96,1536]{1,0:T(8,128)}, u32[]{:S(2)}, u32[]{:S(2)}) collective-permute-start(f32[96,1536]{1,0:T(8,128)} %fusion.45), channel_id=1, source_target_pairs={{0,16},{16,0},{1,17},{17,1},{2,18},{18,2},{3,19},{19,3},{4,20},{20... | collective-permute-start | bytes 1769480 | tf_op jit(solution)/shard_map/ppermute | solution.py:165
  251.6 11.4 %collective-permute-start.51 = (bf16[4,96,768]{2,1,0:T(8,128)(2,1)S(1)}, bf16[4,96,768]{2,1,0:T(8,128)(2,1)S(1)}, u32[]{:S(2)}, u32[]{:S(2)}) collective-permute-start(bf16[4,96,768]{2,1,0:T(8,128)(2,1)S(1)} %fusion.33), channel_id=1, source_target_pairs={{0,16},{16,0},{1,17},{17,1},{2,18},{18,2},{3,19},{19,3},{4,20},{20... | collective-permute-start | bytes 1769480 | tf_op jit(solution)/shard_map/ppermute | solution.py:165
  251.8 8.5 %collective-permute-start.35 = (bf16[384,384]{1,0:T(8,128)(2,1)}, bf16[384,384]{1,0:T(8,128)(2,1)S(1)}, u32[]{:S(2)}, u32[]{:S(2)}) collective-permute-start(bf16[384,384]{1,0:T(8,128)(2,1)} %add_convert_fusion.4), channel_id=1, source_target_pairs={{0,2},{1,3},{2,0},{3,1},{4,6},{5,7},{6,4},{7,5},{8,10},{9,11},{10,... | collective-permute-start | bytes 884744 | tf_op jit(solution)/shard_map/ppermute | solution.py:165
  253.1 8.5 %collective-permute-start.36 = (bf16[384,384]{1,0:T(8,128)(2,1)}, bf16[384,384]{1,0:T(8,128)(2,1)S(1)}, u32[]{:S(2)}, u32[]{:S(2)}) collective-permute-start(bf16[384,384]{1,0:T(8,128)(2,1)} %add_convert_fusion.3), channel_id=1, source_target_pairs={{0,1},{1,0},{2,3},{3,2},{4,5},{5,4},{6,7},{7,6},{8,9},{9,8},{10,11... | collective-permute-start | bytes 884744 | tf_op jit(solution)/shard_map/ppermute | solution.py:165
  255.5 18.4 %collective-permute-start.37 = (bf16[768,384]{1,0:T(8,128)(2,1)S(1)}, bf16[768,384]{1,0:T(8,128)(2,1)S(1)}, u32[]{:S(2)}, u32[]{:S(2)}) collective-permute-start(bf16[768,384]{1,0:T(8,128)(2,1)S(1)} %convolution_convert_fusion.1), channel_id=1, source_target_pairs={{0,1},{1,0},{2,3},{3,2},{4,5},{5,4},{6,7},{7,6},{8,9},{9,8},{10,11... | collective-permute-start | bytes 1769480 | tf_op jit(solution)/shard_map/ppermute | solution.py:165
  260.3 16.6 %collective-permute-start.38 = (bf16[768,384]{1,0:T(8,128)(2,1)S(1)}, bf16[768,384]{1,0:T(8,128)(2,1)S(1)}, u32[]{:S(2)}, u32[]{:S(2)}) collective-permute-start(bf16[768,384]{1,0:T(8,128)(2,1)S(1)} %convolution_convert_fusion), channel_id=1, source_target_pairs={{0,2},{1,3},{2,0},{3,1},{4,6},{5,7},{6,4},{7,5},{8,10},{9,11},{10,... | collective-permute-start | bytes 1769480 | tf_op jit(solution)/shard_map/ppermute | solution.py:165
  263.2 18.7 %collective-permute-start.52 = (bf16[96,768]{1,0:T(8,128)(2,1)S(1)}, bf16[96,768]{1,0:T(8,128)(2,1)S(1)}, u32[]{:S(2)}, u32[]{:S(2)}) collective-permute-start(bf16[96,768]{1,0:T(8,128)(2,1)S(1)} %get-tuple-element.120), channel_id=1, source_target_pairs={{0,4},{4,0},{8,12},{12,8},{1,5},{5,1},{9,13},{13,9},{2,6},{6,2},{1... | collective-permute-start | bytes 442376 | tf_op jit(solution)/shard_map/ppermute | solution.py:165
  263.4 18.6 %collective-permute-start.53 = (bf16[96,768]{1,0:T(8,128)(2,1)S(1)}, bf16[96,768]{1,0:T(8,128)(2,1)S(1)}, u32[]{:S(2)}, u32[]{:S(2)}) collective-permute-start(bf16[96,768]{1,0:T(8,128)(2,1)S(1)} %get-tuple-element.122), channel_id=1, source_target_pairs={{0,8},{4,12},{8,0},{12,4},{1,9},{5,13},{9,1},{13,5},{2,10},{6,14},... | collective-permute-start | bytes 442376 | tf_op jit(solution)/shard_map/ppermute | solution.py:165
  273.9 8.1 %collective-permute-start.54 = (bf16[96,768]{1,0:T(8,128)(2,1)S(1)}, bf16[96,768]{1,0:T(8,128)(2,1)S(1)}, u32[]{:S(2)}, u32[]{:S(2)}) collective-permute-start(bf16[96,768]{1,0:T(8,128)(2,1)S(1)} %get-tuple-element.121), channel_id=1, source_target_pairs={{0,12},{4,8},{8,4},{12,0},{1,13},{5,9},{9,5},{13,1},{2,14},{6,10},... | collective-permute-start | bytes 442376 | tf_op jit(solution)/shard_map/ppermute | solution.py:165
  276.9 7.6 %collective-permute-start.39 = (bf16[384,384]{1,0:T(8,128)(2,1)S(1)}, bf16[384,384]{1,0:T(8,128)(2,1)S(1)}, u32[]{:S(2)}, u32[]{:S(2)}) collective-permute-start(bf16[384,384]{1,0:T(8,128)(2,1)S(1)} %fusion.10), channel_id=1, source_target_pairs={{0,2},{1,3},{2,0},{3,1},{4,6},{5,7},{6,4},{7,5},{8,10},{9,11},{10,... | collective-permute-start | bytes 884744 | tf_op jit(solution)/shard_map/ppermute | solution.py:165
  277.8 6.7 %collective-permute-start.40 = (bf16[384,384]{1,0:T(8,128)(2,1)S(1)}, bf16[384,384]{1,0:T(8,128)(2,1)S(1)}, u32[]{:S(2)}, u32[]{:S(2)}) collective-permute-start(bf16[384,384]{1,0:T(8,128)(2,1)S(1)} %fusion.11), channel_id=1, source_target_pairs={{0,1},{1,0},{2,3},{3,2},{4,5},{5,4},{6,7},{7,6},{8,9},{9,8},{10,11... | collective-permute-start | bytes 884744 | tf_op jit(solution)/shard_map/ppermute | solution.py:165
  282.1 26.2 %collective-permute-start.55 = (f32[96,768]{1,0:T(8,128)S(1)}, f32[96,768]{1,0:T(8,128)}, u32[]{:S(2)}, u32[]{:S(2)}) collective-permute-start(f32[96,768]{1,0:T(8,128)S(1)} %fusion.81), channel_id=1, source_target_pairs={{0,16},{16,0},{1,17},{17,1},{2,18},{18,2},{3,19},{19,3},{4,20},{20... | collective-permute-start | bytes 884744 | tf_op jit(solution)/shard_map/ppermute | solution.py:165
  297.7 9.4 %collective-permute-start.47 = (f32[5952]{0:T(1024)S(1)}, f32[5952]{0:T(1024)S(1)}, u32[]{:S(2)}, u32[]{:S(2)}) collective-permute-start(f32[5952]{0:T(1024)S(1)} %add_add_fusion.1), channel_id=1, source_target_pairs={{0,16},{16,0},{1,17},{17,1},{2,18},{18,2},{3,19},{19,3},{4,20},{20... | collective-permute-start | bytes 71432 | tf_op jit(solution)/shard_map/ppermute | solution.py:165
  (78 other events, 581.7 us)
Sparse Core Ops, SparseCore 0:
  10.3 37.6 all-gather.1
